TPU v7x, 32 devices: a whole 2x2x4 slice. The times are simulated.
32 devices in a mesh: tests: 8 (over z, x), branches: 4 (over y, core).
Axes of the slice: x: 2, y: 2, z: 4, core: 2. Of those that a mesh axis runs over, the one named last changes fastest.
Arguments:
- select: float32 [131072], P('tests'), may hold values from 1e-05 to 0.95
- tiles: float32 [2048, 128, 128], P(('tests', 'branches')), may hold values from 0.0001 to 0.9
- row_block: int32 [2048], P(('tests', 'branches')), may hold values from 0 to 127
- col_block: int32 [2048], P(('tests', 'branches')), may hold values from 0 to 2047, as said below
- counts: int32 [32], P(('tests', 'branches')), may hold values from 1 to 64, 1280 in all
- weights: float32 [1048576], P('branches'), may hold values from 1 to 16
Outputs:
- grad_tests: float32 [131072], P('tests')
- tile_grads: float32 [2048, 128, 128], P(('tests', 'branches'))
- next_select: float32 [131072], P('tests')
Inputs may be any that keep to these rules, and one draw needn't show every extreme that they name: counts[d] is the number of device d's slots, from its first, that hold tiles. Call col_block[s] // 256 the share of slot s. Of the 64 slots of one device at most 12 have one share; in every index of branches one share holds exactly 12 slots of every device there.
All inputs are finite; a program needn't handle non-finite values.
Results may differ from a plain program's by a relative error of at most 0.0003.
Values sent between devices are 32-bit elements; how exact they have to be, the bound alone decides.
No kernel may reach another device: no remote copies, remote signals or barrier semaphores. Data moves between devices by JAX's collectives and lax.ppermute only.
A program may use at most 64 MiB of HBM per device.

v0:
```python
import jax
import jax.numpy as jnp
from jax import lax
from jax.sharding import PartitionSpec as P

STEPS = 2


ascent_rate = 0.0015
select_cap = 0.5


def tile_logs(blocks, tiles, rows, live):
    picked = blocks[rows]
    logs = jnp.sum(jnp.log1p(-picked[:, :, None] * tiles), axis=1)
    return jnp.where(live[:, None], logs, jnp.zeros_like(logs))


def tile_terms(blocks, slot_survive, tiles, rows, live):
    picked = blocks[rows]
    inverse = 1.0 / (1.0 - picked[:, :, None] * tiles)
    scaled = slot_survive[:, None, :] * inverse
    tests_part = jnp.sum(scaled * tiles, axis=2)
    tests_part = jnp.where(live[:, None], tests_part, jnp.zeros_like(tests_part))
    tile_part = scaled * picked[:, :, None]
    tile_part = jnp.where(live[:, None, None], tile_part, jnp.zeros_like(tile_part))
    return (tests_part, tile_part)


def body(select, tiles, row_block, col_block, counts, weights):
    width = tiles.shape[1]
    slots = tiles.shape[0]
    test_rows = select.shape[0] // width
    branch_rows = weights.shape[0] // width
    weight_rows = weights.reshape(branch_rows, width)
    limit = counts[0]
    current = select
    grad_tests = select
    tile_grads = tiles
    for step in range(STEPS):
        keep = step == STEPS - 1
        blocks = current.reshape(test_rows, width)
        live = jnp.arange(slots, dtype=jnp.int32) < limit
        slot_logs = tile_logs(blocks, tiles, row_block, live)
        partial_value = jnp.zeros((branch_rows, width), jnp.float32).at[col_block].add(slot_logs)
        summed = lax.psum(partial_value, "tests")
        slot_survive = (weight_rows * jnp.exp(summed))[col_block]
        empty_tests = jnp.zeros((test_rows, width), jnp.float32)
        live = jnp.arange(slots, dtype=jnp.int32) < limit
        tests_part, tile_part = tile_terms(blocks, slot_survive, tiles, row_block, live)
        tests_sum = empty_tests.at[row_block].add(tests_part)
        gradient = lax.psum(tests_sum, "branches").reshape(-1)
        if keep:
            grad_tests = gradient
            tile_grads = tile_part
        rate = ascent_rate * gradient
        current = current + (select_cap - current) * rate / (1.0 + rate)
    return (grad_tests, tile_grads, current)


def solution(mesh):
    return jax.shard_map(
        body,
        mesh=mesh,
        in_specs=(
            P("tests"),
            P(("tests", "branches"), None, None),
            P(("tests", "branches")),
            P(("tests", "branches")),
            P(("tests", "branches")),
            P("branches"),
        ),
        out_specs=(P("tests"), P(("tests", "branches"), None, None), P("tests")),
        check_vma=False,
    )
```

profile of v0, /device:TPU:0, one launch (start us, length us, event | category | flops | bytes accessed | tf_op | source)
XLA Modules:
  0.0 270.3 jit_solution(17124041052368944611)
XLA Ops:
  7.2 0.0 copy-start
  7.2 0.0 all-reduce.5.cloned.1.call-start
  8.0 0.7 compare_select_fusion.1
  8.6 0.7 compare_select_fusion
  9.3 1.4 gather_fusion
  10.7 3.3 %log-plus-one_reduce_fusion.1 = f32[64,128]{1,0:T(8,128)S(1)} fusion(f32[64,128,128]{2,1,0:T(8,128)} %param.7, f32[64,128]{1,0:T(8,128)S(1)} %neg.16), kind=kLoop, calls=%fused_computation.13 | loop fusion | flops 2088960 | bytes 4259840 | tf_op jit(solution)/shard_map/reduce_sum | solution.py:15
  14.1 1.9 scatter_custom_fusion
  15.9 0.0 all-reduce.5.cloned.1.call-update
  16.0 0.0 copy-start.1
  16.0 0.0 all-reduce.7.cloned.1.call-start
  16.0 80.8 %all-reduce.5.cloned.1.call-done = f32[2048,128]{1,0:T(8,128)} async-done(((f32[2048,128]{1,0:T(8,128)}), f32[2048,128]{1,0:T(8,128)}) %all-reduce.5.cloned.1.call-update) | async-done | bytes 1048592 | tf_op jit(solution)/shard_map/psum | solution.py:46
  96.8 0.0 copy-done
  96.8 1.4 bitcast_multiply_fusion.1
  98.2 0.6 gather_fusion.1
  98.8 4.5 %multiply_reduce_fusion.1 = f32[64,128]{1,0:T(8,128)S(1)} fusion(f32[64,128,128]{2,1,0:T(8,128)} %param.7, f32[64,128]{1,0:T(8,128)S(1)} %gather_fusion, f32[64,128]{1,0:T(8,128)S(1)} %gather_fusion.1), kind=kLoop, calls=%fused_computation.12 | loop fusion | flops 6283264 | bytes 4292608 | tf_op jit(solution)/shard_map/reduce_sum | solution.py:23
  103.3 1.5 scatter_custom_fusion.1
  104.7 0.0 all-reduce.7.cloned.1.call-update
  104.8 0.0 all-reduce.9.cloned.1.call-start
  104.8 30.8 %all-reduce.7.cloned.1.call-done = f32[128,128]{1,0:T(8,128)} async-done(((f32[128,128]{1,0:T(8,128)}), f32[128,128]{1,0:T(8,128)}) %all-reduce.7.cloned.1.call-update) | async-done | bytes 65552 | tf_op jit(solution)/shard_map/psum | solution.py:52
  135.6 0.0 copy-done.1
  135.6 0.9 fusion.22
  136.4 0.6 gather_fusion.2
  137.0 3.3 %log-plus-one_reduce_fusion = f32[64,128]{1,0:T(8,128)S(1)} fusion(f32[64,128,128]{2,1,0:T(8,128)} %param.7, f32[64,128]{1,0:T(8,128)S(1)} %neg.17), kind=kLoop, calls=%fused_computation.11 | loop fusion | flops 2088960 | bytes 4259840 | tf_op jit(solution)/shard_map/reduce_sum | solution.py:15
  140.4 1.9 scatter_custom_fusion.2
  142.3 0.0 all-reduce.9.cloned.1.call-update
  142.3 0.0 all-reduce.11.cloned.1.call-start
  142.3 78.3 %all-reduce.9.cloned.1.call-done = f32[2048,128]{1,0:T(8,128)} async-done(((f32[2048,128]{1,0:T(8,128)}), f32[2048,128]{1,0:T(8,128)}) %all-reduce.9.cloned.1.call-update) | async-done | bytes 1048592 | tf_op jit(solution)/shard_map/psum | solution.py:46
  220.6 1.4 bitcast_multiply_fusion
  222.0 0.6 gather_fusion.3
  222.6 0.0 copy-start.2
  222.6 5.9 %multiply_select_fusion = (f32[64,128,128]{2,1,0:T(8,128)}, f32[64,128]{1,0:T(8,128)S(1)}) fusion(f32[64,128,128]{2,1,0:T(8,128)} %param.7, f32[64,128]{1,0:T(8,128)S(1)} %gather_fusion.2, f32[64,128]{1,0:T(8,128)S(1)} %gather_fusion.3, pred[64]{0:T(512)(128)(4,1)S(1)} %iota_compare_fusion), kind=kLoop, calls=%fused_computation.8 | loop fusion | flops 8380416 | bytes 8486976 | tf_op jit(solution)/shard_map/jit(_where)/select_n | solution.py:26
  228.5 1.5 scatter_custom_fusion.3
  229.9 0.0 all-reduce.11.cloned.1.call-update
  230.0 30.8 %all-reduce.11.cloned.1.call-done = f32[16384]{0:T(1024)} async-done(((f32[16384]{0:T(1024)}), f32[16384]{0:T(1024)}) %all-reduce.11.cloned.1.call-update) | async-done | bytes 65552 | tf_op jit(solution)/shard_map/psum | solution.py:52
  260.8 0.0 copy-done.2
  260.8 1.5 divide_add_fusion
  262.3 1.5 copy.14
  (5 shorter events, 0.0 us)
Async XLA Ops:
  7.2 89.6 %copy-start = (f32[262144]{0:T(1024)S(1)}, f32[262144]{0:T(1024)}, u32[]{:S(2)}) copy-start(f32[262144]{0:T(1024)} %param.11) | copy-start | bytes 3145732
  7.2 89.6 %all-reduce.5.cloned.1.call-start = ((), (), s32[]{:S(2)}) async-start(), calls=%async_computation | async-start | bytes 2097152 | tf_op jit(solution)/shard_map/psum | solution.py:46
  16.0 119.6 %copy-start.1 = (f32[16384]{0:T(1024)S(1)}, f32[16384]{0:T(1024)}, u32[]{:S(2)}) copy-start(f32[16384]{0:T(1024)} %param.6) | copy-start | bytes 196612
  16.0 119.6 %all-reduce.7.cloned.1.call-start = ((), (), s32[]{:S(2)}) async-start(), calls=%async_computation.1 | async-start | bytes 131072 | tf_op jit(solution)/shard_map/psum | solution.py:52
  104.8 115.9 %all-reduce.9.cloned.1.call-start = ((), (), s32[]{:S(2)}) async-start(), calls=%async_computation.2 | async-start | bytes 2097152 | tf_op jit(solution)/shard_map/psum | solution.py:46
  142.3 118.5 %all-reduce.11.cloned.1.call-start = ((), (), s32[]{:S(2)}) async-start(), calls=%async_computation.3 | async-start | bytes 131072 | tf_op jit(solution)/shard_map/psum | solution.py:52
  222.6 38.2 %copy-start.2 = (f32[128,128]{1,0:T(8,128)S(1)}, f32[128,128]{1,0:T(8,128)}, u32[]{:S(2)}) copy-start(f32[128,128]{1,0:T(8,128)} %all-reduce.7.cloned.1.call-done) | copy-start | bytes 196612
Sparse Core Ops, SparseCore 0:
  16.1 80.6 all-reduce.4
  104.9 30.6 all-reduce.6
  142.4 78.1 all-reduce.8
  230.1 30.6 all-reduce.10
where the time goes:
time: 271 us; the launch traced here: 270 us
  waiting for transfers between devices  221 us (82%)
  other arithmetic  30.2 us (11%)
  between operations  14.6 us (5%)
  local copies, waits for them, and re-layouts  4.71 us (2%)
    psum x2, waiting for transfers between devices, body(): summed = lax.psum(partial_value, 'tests')  159 us
    psum x2, waiting for transfers between devices, body(): gradient = lax.psum(tests_sum, 'branches').reshape(-1)  61.6 us
    reduce_sum x2, other arithmetic, tile_logs(): logs = jnp.sum(jnp.log1p(-picked[:, :, None] * tiles), axis=1)  6.68 us
    select_n x1, other arithmetic, tile_terms(): jnp.where(live[:, None, None], tile_part, jnp.zeros_like(tile_part))  5.88 us
  transfers between devices with their start and end apart: 4, of which 4 were waited for; matrix products, arithmetic and copies ran while one was open for 0% of the time, Pallas kernels for 0%

commit v1 on v0

v1 whole, which is shorter than its diff:
```python
import functools

import jax
import jax.numpy as jnp
from jax import lax
from jax.experimental import pallas as pl
from jax.experimental.pallas import tpu as pltpu
from jax.sharding import PartitionSpec as P

STEPS = 2
GROUP = 8
EXTRA = 8
F32 = jnp.float32
BF16 = jnp.bfloat16

ascent_rate = 0.0015
select_cap = 0.5


def pieces(x):
    high = x.astype(BF16)
    rest = x - high.astype(F32)
    middle = rest.astype(BF16)
    low = (rest - middle.astype(F32)).astype(BF16)
    return high, middle, low


def pick(ones, x):
    total = jnp.zeros((ones.shape[0], x.shape[1]), F32)
    for piece in pieces(x)[::-1]:
        total = total + jnp.dot(ones, piece, preferred_element_type=F32)
    return total


def inverse_of(x):
    guess = pl.reciprocal(x, approx=True)
    return guess * (2.0 - x * guess)


def spread(values, count, width, fill):
    rows = [jnp.full((1, width), values[s], jnp.int32) for s in range(count)]
    rows.append(jnp.full((width - count, width), fill, jnp.int32))
    return jnp.concatenate(rows, axis=0)


def pick_columns(rows, blocks, picked, columns):
    slots = rows.shape[0]
    for s in range(slots):
        picked[pl.ds(s, 1), :] = blocks[pl.ds(rows[s], 1), :]
    columns[...] = picked[...].T


def shifted(columns, group):
    width = columns.shape[1]
    return pltpu.roll(columns[...], lax.rem(width - group * GROUP, width), 1)


def slot_pass(group, limit, columns, tiles, ratios, logs):
    now = shifted(columns, group)
    for i in range(GROUP):
        s = group * GROUP + i
        tile = tiles[s]
        left = 1.0 - now[:, i : i + 1] * tile
        ratios[s] = tile * inverse_of(left)
        product = left[:8]
        for at in range(8, left.shape[0], 8):
            product = product * left[at : at + 8]
        row = jnp.sum(jnp.log(product), axis=0, keepdims=True)
        logs[pl.ds(s, 1), :] = jnp.where(s < limit, row, jnp.zeros_like(row))


def first_kernel(limit, rows, cols, blocks, tiles, weights, payload, ratios, held, slot_weights, picked, columns, tile_sem, weight_sem):
    slots, width = held.shape[0], held.shape[1]
    groups = slots // GROUP

    def tile_copy(group):
        part = pl.ds(group * GROUP, GROUP)
        return pltpu.make_async_copy(tiles.at[part], held.at[part], tile_sem.at[group])

    def weight_copy(s):
        return pltpu.make_async_copy(weights.at[pl.ds(cols[s], 1)], slot_weights.at[pl.ds(s, 1)], weight_sem)

    for group in range(groups):
        tile_copy(group).start()
    for s in range(slots):
        weight_copy(s).start()
    picked[...] = jnp.zeros_like(picked)
    pick_columns(rows, blocks, picked, columns)
    payload[pl.ds(slots, EXTRA), :] = spread(cols, slots, width, -1).T[:EXTRA].astype(F32)

    def step(group, carry):
        tile_copy(group).wait()
        slot_pass(group, limit[0], columns, held, ratios, payload)
        return carry

    lax.fori_loop(0, groups, step, 0)
    pltpu.make_async_copy(weights.at[pl.ds(0, slots)], slot_weights, weight_sem).wait()


def survive(limit, cols, gathered, others, slot_weights):
    slots, width = slot_weights.shape
    mine = jnp.concatenate([jnp.full((1, width), cols[s], jnp.int32) for s in range(slots)], axis=0).astype(F32)
    total = jnp.zeros((slots, width), F32)
    for j in range(gathered.shape[0]):
        same = jnp.where(mine == others[j, pl.ds(slots, 1), :], 1.0, 0.0).astype(BF16)
        total = total + pick(same[:, :slots], gathered[j, pl.ds(0, slots), :])
    live = lax.broadcasted_iota(jnp.int32, (slots, width), 0) < limit[0]
    return jnp.where(live, slot_weights[...] * jnp.exp(total), 0.0)


def tests_sums(rows, survival, ratios):
    slots, width = survival.shape
    lanes = lax.broadcasted_iota(jnp.int32, (width, width), 1)

    def step(group, total):
        for i in range(GROUP):
            s = group * GROUP + i
            terms = jnp.sum(ratios[s] * survival[pl.ds(s, 1), :], axis=1, keepdims=True)
            total = jnp.where(lanes == s, terms, total)
        return total

    sums = lax.fori_loop(0, slots // GROUP, step, jnp.zeros((width, width), F32)).T
    targets = spread(rows, slots, width, -1).T
    hits = jnp.where(targets == lax.broadcasted_iota(jnp.int32, (width, width), 0), 1.0, 0.0).astype(BF16)
    return pick(hits, sums)


def gradient_kernel(limit, rows, cols, gathered, others, slot_weights, ratios, partial, survival):
    survival[...] = survive(limit, cols, gathered, others, slot_weights)
    partial[...] = tests_sums(rows, survival, ratios)


def advance(current, gradient):
    rate = ascent_rate * gradient
    return current + (select_cap - current) * rate / (1.0 + rate)


def total_of(parts):
    while len(parts) > 1:
        parts = [a + b for a, b in zip(parts[::2], parts[1::2])]
    return parts[0]


def next_kernel(limit, rows, blocks, held, *refs):
    *partials, current, logs, ratios, picked, columns = refs
    current[...] = advance(blocks[...], total_of([p[...] for p in partials]))
    picked[...] = jnp.zeros_like(picked)
    pick_columns(rows, current, picked, columns)

    def step(group, carry):
        slot_pass(group, limit[0], columns, held, ratios, logs)
        return carry

    lax.fori_loop(0, held.shape[0] // GROUP, step, 0)


def tile_kernel(rows, blocks, survival, held, out, picked, columns):
    group = pl.program_id(0)

    @pl.when(group == 0)
    def _():
        picked[...] = jnp.zeros_like(picked)
        pick_columns(rows, blocks, picked, columns)

    now = shifted(columns, group)
    for i in range(GROUP):
        s = group * GROUP + i
        share = now[:, i : i + 1]
        out[i] = survival[pl.ds(s, 1), :] * share * inverse_of(1.0 - share * held[s])


SMEM = pl.BlockSpec(memory_space=pltpu.SMEM)
VMEM = pl.BlockSpec(memory_space=pltpu.VMEM)
ANY = pl.BlockSpec(memory_space=pl.ANY)
PARAMS = pltpu.CompilerParams(vmem_limit_bytes=24 << 20)


def body(tests, branches, select, tiles, row_block, col_block, counts, weights):
    slots, width = tiles.shape[0], tiles.shape[1]
    blocks = select.reshape(-1, width)
    weight_rows = weights.reshape(-1, width)
    test_rows = blocks.shape[0]
    square = pltpu.VMEM((width, width), F32)
    full = jax.ShapeDtypeStruct(tiles.shape, F32)
    per_slot = jax.ShapeDtypeStruct((slots, width), F32)
    per_test = jax.ShapeDtypeStruct((test_rows, width), F32)

    def over_tests(x):
        return lax.all_to_all(jnp.broadcast_to(x[None], (tests,) + x.shape), "tests", 0, 0)

    def over_branches(x):
        return [x] + [lax.ppermute(x, "branches", [(b, b ^ k) for b in range(branches)]) for k in range(1, branches)]

    payload, ratios, held, slot_weights = pl.pallas_call(
        first_kernel,
        out_shape=(jax.ShapeDtypeStruct((slots + EXTRA, width), F32), full, full, per_slot),
        in_specs=[SMEM, SMEM, SMEM, VMEM, ANY, ANY],
        out_specs=(VMEM,) * 4,
        scratch_shapes=[square, square, pltpu.SemaphoreType.DMA((slots // GROUP,)), pltpu.SemaphoreType.DMA],
        compiler_params=PARAMS,
        name="first_logs",
    )(counts, row_block, col_block, blocks, tiles, weight_rows)
    others = over_tests(payload)
    gathered = others
    current = blocks
    for step in range(STEPS):
        partial, survival = pl.pallas_call(
            gradient_kernel,
            out_shape=(per_test, per_slot),
            in_specs=[SMEM, SMEM, SMEM, VMEM, VMEM, VMEM, VMEM],
            out_specs=(VMEM, VMEM),
            compiler_params=PARAMS,
            name="gradient",
        )(counts, row_block, col_block, gathered, others, slot_weights, ratios)
        partials = over_branches(partial)
        if step < STEPS - 1:
            current, logs, ratios = pl.pallas_call(
                next_kernel,
                out_shape=(per_test, per_slot, full),
                in_specs=[SMEM, SMEM, VMEM, VMEM] + [VMEM] * branches,
                out_specs=(VMEM,) * 3,
                scratch_shapes=[square, square],
                compiler_params=PARAMS,
                name="next_logs",
            )(counts, row_block, current, held, *partials)
            gathered = over_tests(logs)
    tile_grads = pl.pallas_call(
        tile_kernel,
        grid=(slots // GROUP,),
        out_shape=full,
        in_specs=[SMEM, VMEM, VMEM, VMEM],
        out_specs=pl.BlockSpec((GROUP, width, width), lambda i: (i, 0, 0)),
        scratch_shapes=[square, square],
        compiler_params=PARAMS,
        name="tile_gradients",
    )(row_block, current, survival, held)
    gradient = total_of(partials)
    return gradient.reshape(-1), tile_grads, advance(current, gradient).reshape(-1)


def solution(mesh):
    return jax.shard_map(
        functools.partial(body, mesh.shape["tests"], mesh.shape["branches"]),
        mesh=mesh,
        in_specs=(
            P("tests"),
            P(("tests", "branches"), None, None),
            P(("tests", "branches")),
            P(("tests", "branches")),
            P(("tests", "branches")),
            P("branches"),
        ),
        out_specs=(P("tests"), P(("tests", "branches"), None, None), P("tests")),
        check_vma=False,
    )
```

time: 271 us -> 63.5 us (0.23)
  waiting for transfers between devices: 221 us -> 3.94 us
  other arithmetic: 30.2 us -> 0.68 us
  blocking collectives: 0 us -> 29.2 us
  Pallas kernels: 0 us -> 18.5 us
  between operations: 14.6 us -> 1.36 us
  starting transfers between devices: 0.16 us -> 3.78 us
    psum x4 -> x0, waiting for transfers between devices: 221 us -> none  [the longest x2 159 us: body(): summed = lax.psum(partial_value, 'tests')]
    all_to_all x0 -> x2, blocking collectives: none -> 29.2 us  [over_tests(): lax.all_to_all(jnp.broadcast_to(x[None], (tests,) + x.shape), 'tests', 0, 0)]
    pallas_call x0 -> x5, Pallas kernels: none -> 18.5 us  [the longest x2 5.97 us: body(): pl.pallas_call(gradient_kernel, out_shape=(per_test, per_slot), in_specs=...]
    reduce_sum x3 -> x0, other arithmetic: 11.2 us -> none  [the longest x2 6.68 us: tile_logs(): logs = jnp.sum(jnp.log1p(-picked[:, :, None] * tiles), axis=1)]
    select_n x3 -> x0, other arithmetic: 7.2 us -> none  [the longest x1 5.88 us: tile_terms(): jnp.where(live[:, None, None], tile_part, jnp.zeros_like(tile_part))]
    scatter-add x4 -> x0, other arithmetic: 6.65 us -> none  [the longest x2 3.73 us: body(): jnp.zeros((branch_rows, width), jnp.float32).at[col_block].add(slot_logs)]
    unnamed x7 -> x14, local copies, waits for them, and re-layouts: 1.49 us -> 5.56 us
    ppermute x0 -> x6, waiting for transfers between devices: none -> 3.94 us  [over_branches(): lax.ppermute(x, 'branches', [(b, b ^ k) for b in range(branches)])]
  transfers between devices with their start and end apart: 4 -> 6, of which waited for: 4 -> 2; matrix products, arithmetic and copies ran while one was open for 0% -> 0% of each run, Pallas kernels for 0% -> 9%
where the time goes in v1:
time: 63.5 us; the launch traced here: 63.1 us
  blocking collectives  29.2 us (46%)
  Pallas kernels  18.5 us (29%)
  local copies, waits for them, and re-layouts  5.6 us (9%)
  waiting for transfers between devices  3.94 us (6%)
  starting transfers between devices  3.78 us (6%)
  between operations  1.36 us (2%)
  other arithmetic  0.68 us (1%)
    all_to_all x2, blocking collectives, over_tests(): lax.all_to_all(jnp.broadcast_to(x[None], (tests,) + x.shape), 'tests', 0, 0)  29.2 us
    pallas_call x2, Pallas kernels, body(): pl.pallas_call(gradient_kernel, out_shape=(per_test, per_slot), in_specs=...  5.97 us
    unnamed x14, local copies, waits for them, and re-layouts  5.56 us
    pallas_call x1, Pallas kernels, body(): pl.pallas_call(tile_kernel, grid=(slots // GROUP,), out_shape=full, in_sp...  5.41 us
    ppermute x6, waiting for transfers between devices, over_branches(): lax.ppermute(x, 'branches', [(b, b ^ k) for b in range(branches)])  3.94 us
    pallas_call x1, Pallas kernels, body(): pl.pallas_call(first_kernel, out_shape=(jax.ShapeDtypeStruct((slots + EXT...  3.9 us
    ppermute x6, starting transfers between devices, over_branches(): lax.ppermute(x, 'branches', [(b, b ^ k) for b in range(branches)])  3.78 us
    pallas_call x1, Pallas kernels, body(): pl.pallas_call(next_kernel, out_shape=(per_test, per_slot, full), in_spec...  3.24 us
  transfers between devices with their start and end apart: 6, of which 2 were waited for; matrix products, arithmetic and copies ran while one was open for 0% of the time, Pallas kernels for 9%

profile of v1, /device:TPU:0, one launch (start us, length us, event | category | flops | bytes accessed | tf_op | source)
XLA Modules:
  0.0 63.1 jit_solution(18183788880565501884)
XLA Ops:
  1.3 0.0 copy-start
  1.3 2.2 %copy-done = f32[64,128,128]{2,1,0:T(8,128)S(1)} copy-done((f32[64,128,128]{2,1,0:T(8,128)S(1)}, f32[64,128,128]{2,1,0:T(8,128)}, u32[]{:S(2)}) %copy-start) | copy-done | bytes 4194328
  3.5 0.0 copy-start.1
  3.5 1.2 %copy-done.1 = f32[262144]{0:T(1024)S(1)} copy-done((f32[262144]{0:T(1024)S(1)}, f32[262144]{0:T(1024)}, u32[]{:S(2)}) %copy-start.1) | copy-done | bytes 1048600
  4.7 0.0 copy-start.2
  4.7 0.8 %copy-done.2 = f32[16384]{0:T(1024)S(1)} copy-done((f32[16384]{0:T(1024)S(1)}, f32[16384]{0:T(1024)}, u32[]{:S(2)}) %copy-start.2) | copy-done | bytes 65560
  5.5 0.0 copy-start.4
  5.5 0.7 %copy-done.4 = s32[64]{0:T(128)S(1)} copy-done((s32[64]{0:T(128)S(1)}, s32[64]{0:T(128)}, u32[]{:S(2)}) %copy-start.4) | copy-done | bytes 280
  6.2 0.0 copy-start.5
  6.2 0.7 %copy-done.5 = s32[64]{0:T(128)S(1)} copy-done((s32[64]{0:T(128)S(1)}, s32[64]{0:T(128)}, u32[]{:S(2)}) %copy-start.5) | copy-done | bytes 280
  6.8 3.9 %first_logs.1 = (f32[72,128]{1,0:T(8,128)S(1)}, f32[64,128,128]{2,1,0:T(8,128)S(1)}, f32[64,128,128]{2,1,0:T(8,128)S(1)}, f32[64,128]{1,0:T(8,128)S(1)}) custom-call(s32[1]{0:T(128)S(6)} %copy.9.limit, s32[64]{0:T(128)S(1)} %copy-done.4, s32[64]{0:T(128)S(1)} %copy-done.5, f32[128,128]{1,0:T(8,128)S(1)} %bitcast.6, f32[64,128,128]{2,1,0:T(8,128)S(1)} %copy-done, ...), custom_call_target="tpu_custom_call" | custom-call | tf_op jit(solution)/shard_map/first_logs/pallas_call | solution.py:194
  10.8 0.0 copy-start.3
  10.8 17.4 %all_to_all.10.gathered.others = f32[8,72,128]{2,1,0:T(8,128)S(1)} all-to-all(f32[8,72,128]{2,1,0:T(8,128)S(1)} %broadcast_in_dim.4), channel_id=1, replica_groups=mesh['tests'=8,'branches'=4] {'tests'}, dimensions={0} | all-to-all | bytes 589824 | tf_op jit(solution)/shard_map/all_to_all | solution.py:189
  28.2 0.0 copy-start.6
  28.2 3.2 %gradient.2 = (f32[128,128]{1,0:T(8,128)S(1)}, f32[64,128]{1,0:T(8,128)}) custom-call(s32[1]{0:T(128)S(6)} %copy.9.limit, s32[64]{0:T(128)S(1)} %copy-done.4, s32[64]{0:T(128)S(1)} %copy-done.5, f32[8,72,128]{2,1,0:T(8,128)S(1)} %all_to_all.10.gathered.others, f32[8,72,128]{2,1,0:T(8,128)S(1)} %all_to_all.10.gathered.others, ...), custom_call_target="tpu_custom_call" | custom-call | tf_op jit(solution)/shard_map/gradient/pallas_call | solution.py:207
  31.4 0.0 collective-permute-start.2
  31.4 1.6 %collective-permute-start.1 = (f32[128,128]{1,0:T(8,128)S(1)}, f32[128,128]{1,0:T(8,128)S(1)}, u32[]{:S(2)}, u32[]{:S(2)}) collective-permute-start(f32[128,128]{1,0:T(8,128)S(1)} %get-tuple-element.17.refs_0_), channel_id=1, source_target_pairs={{0,2},{1,3},{2,0},{3,1},{4,6},{5,7},{6,4},{7,5},{8,10},{9,11},{10,... | collective-permute-start | bytes 196616 | tf_op jit(solution)/shard_map/ppermute | solution.py:192
  32.9 0.3 collective-permute-start
  33.2 2.5 %collective-permute-done.2.refs_3_ = f32[128,128]{1,0:T(8,128)S(1)} collective-permute-done((f32[128,128]{1,0:T(8,128)S(1)}, f32[128,128]{1,0:T(8,128)S(1)}, u32[]{:S(2)}, u32[]{:S(2)}) %collective-permute-start.2) | collective-permute-done | bytes 65568 | tf_op jit(solution)/shard_map/ppermute | solution.py:192
  35.7 1.5 %collective-permute-done.1.refs_2_ = f32[128,128]{1,0:T(8,128)S(1)} collective-permute-done((f32[128,128]{1,0:T(8,128)S(1)}, f32[128,128]{1,0:T(8,128)S(1)}, u32[]{:S(2)}, u32[]{:S(2)}) %collective-permute-start.1) | collective-permute-done | bytes 65568 | tf_op jit(solution)/shard_map/ppermute | solution.py:192
  37.2 0.0 collective-permute-done.refs_1_
  37.2 0.0 copy-done.3
  37.2 3.2 %next_logs.1 = (f32[128,128]{1,0:T(8,128)S(1)}, f32[64,128]{1,0:T(8,128)S(1)}, f32[64,128,128]{2,1,0:T(8,128)S(1)}) custom-call(s32[1]{0:T(128)S(6)} %copy.9.limit, s32[64]{0:T(128)S(1)} %copy-done.4, f32[128,128]{1,0:T(8,128)S(1)} %bitcast.7, f32[64,128,128]{2,1,0:T(8,128)S(1)} %get-tuple-element.13.held, f32[128,128]{1,0:T(8,128)S(1)} %get-tuple-element.17.refs_0_, ...), custom_call_target="tpu_custom_call" | custom-call | tf_op jit(solution)/shard_map/next_logs/pallas_call | solution.py:217
  40.4 11.8 %all_to_all.11.gathered = f32[8,64,128]{2,1,0:T(8,128)S(1)} all-to-all(f32[8,64,128]{2,1,0:T(8,128)S(1)} %broadcast_in_dim.5), channel_id=1, replica_groups=mesh['tests'=8,'branches'=4] {'tests'}, dimensions={0} | all-to-all | bytes 524288 | tf_op jit(solution)/shard_map/all_to_all | solution.py:189
  52.3 0.0 copy-done.6
  52.3 2.8 %gradient.3 = (f32[128,128]{1,0:T(8,128)S(1)}, f32[64,128]{1,0:T(8,128)S(1)}) custom-call(s32[1]{0:T(128)S(6)} %copy.9.limit, s32[64]{0:T(128)S(1)} %copy-done.4, s32[64]{0:T(128)S(1)} %copy-done.6, f32[8,64,128]{2,1,0:T(8,128)S(1)} %all_to_all.11.gathered, f32[8,72,128]{2,1,0:T(8,128)S(1)} %all_to_all.10.gathered.others, ...), custom_call_target="tpu_custom_call" | custom-call | tf_op jit(solution)/shard_map/gradient/pallas_call | solution.py:207
  55.1 0.1 collective-permute-start.5
  55.1 1.3 %collective-permute-start.4 = (f32[128,128]{1,0:T(8,128)S(1)}, f32[128,128]{1,0:T(8,128)S(1)}, u32[]{:S(2)}, u32[]{:S(2)}) collective-permute-start(f32[128,128]{1,0:T(8,128)S(1)} %get-tuple-element.20), channel_id=1, source_target_pairs={{0,2},{1,3},{2,0},{3,1},{4,6},{5,7},{6,4},{7,5},{8,10},{9,11},{10,... | collective-permute-start | bytes 196616 | tf_op jit(solution)/shard_map/ppermute | solution.py:192
  56.5 0.5 collective-permute-start.3
  57.0 5.4 %tile_gradients.1 = f32[64,128,128]{2,1,0:T(8,128)} custom-call(s32[64]{0:T(128)S(1)} %copy-done.4, f32[128,128]{1,0:T(8,128)S(1)} %get-tuple-element.21.blocks, f32[64,128]{1,0:T(8,128)S(1)} %get-tuple-element.22.survival, f32[64,128,128]{2,1,0:T(8,128)S(1)} %get-tuple-element.13.held), custom_call_target="tpu_custom_call" | custom-call | tf_op jit(solution)/shard_map/tile_gradients/pallas_call | solution.py:227
  62.4 0.0 collective-permute-done.5
  62.4 0.0 collective-permute-done.4
  62.4 0.0 collective-permute-done.3
  62.4 0.7 %add_bitcast_fusion = (f32[16384]{0:T(1024)}, f32[128,128]{1,0:T(8,128)}) fusion(f32[128,128]{1,0:T(8,128)S(1)} %get-tuple-element.21.blocks, f32[128,128]{1,0:T(8,128)S(1)} %collective-permute-done.4, f32[128,128]{1,0:T(8,128)S(1)} %collective-permute-done.5, f32[128,128]{1,0:T(8,128)S(1)} %get-tuple-element.20, f32[128,128]{1,0:T(8,128)S(1)} %collective-permute-done.3), kind=kLoop, calls=%fused_computation | loop fusion | flops 147456 | bytes 458752 | tf_op jit(solution)/shard_map/reshape | solution.py:238
  (2 shorter events, 0.0 us)
Async XLA Ops:
  1.3 2.2 %copy-start = (f32[64,128,128]{2,1,0:T(8,128)S(1)}, f32[64,128,128]{2,1,0:T(8,128)}, u32[]{:S(2)}) copy-start(f32[64,128,128]{2,1,0:T(8,128)} %tiles.1) | copy-start | bytes 12582916
  3.5 1.2 %copy-start.1 = (f32[262144]{0:T(1024)S(1)}, f32[262144]{0:T(1024)}, u32[]{:S(2)}) copy-start(f32[262144]{0:T(1024)} %param.11) | copy-start | bytes 3145732
  4.7 0.8 %copy-start.2 = (f32[16384]{0:T(1024)S(1)}, f32[16384]{0:T(1024)}, u32[]{:S(2)}) copy-start(f32[16384]{0:T(1024)} %param.6) | copy-start | bytes 196612
  5.5 0.7 %copy-start.4 = (s32[64]{0:T(128)S(1)}, s32[64]{0:T(128)}, u32[]{:S(2)}) copy-start(s32[64]{0:T(128)} %rows.9) | copy-start | bytes 772
  6.2 0.7 %copy-start.5 = (s32[64]{0:T(128)S(1)}, s32[64]{0:T(128)}, u32[]{:S(2)}) copy-start(s32[64]{0:T(128)} %cols.5) | copy-start | bytes 772
  10.8 26.4 %copy-start.3 = (f32[16384]{0:T(1024)S(1)}, f32[16384]{0:T(1024)}, u32[]{:S(2)}) copy-start(f32[16384]{0:T(1024)} %param.6) | copy-start | bytes 196612
  28.2 24.1 %copy-start.6 = (s32[64]{0:T(128)S(1)}, s32[64]{0:T(128)}, u32[]{:S(2)}) copy-start(s32[64]{0:T(128)} %cols.5) | copy-start | bytes 772
  31.4 4.3 %collective-permute-start.2 = (f32[128,128]{1,0:T(8,128)S(1)}, f32[128,128]{1,0:T(8,128)S(1)}, u32[]{:S(2)}, u32[]{:S(2)}) collective-permute-start(f32[128,128]{1,0:T(8,128)S(1)} %get-tuple-element.17.refs_0_), channel_id=1, source_target_pairs={{0,3},{1,2},{2,1},{3,0},{4,7},{5,6},{6,5},{7,4},{8,11},{9,10},{10,... | collective-permute-start | bytes 196616 | tf_op jit(solution)/shard_map/ppermute | solution.py:192
  31.4 5.8 %collective-permute-start.1 = (f32[128,128]{1,0:T(8,128)S(1)}, f32[128,128]{1,0:T(8,128)S(1)}, u32[]{:S(2)}, u32[]{:S(2)}) collective-permute-start(f32[128,128]{1,0:T(8,128)S(1)} %get-tuple-element.17.refs_0_), channel_id=1, source_target_pairs={{0,2},{1,3},{2,0},{3,1},{4,6},{5,7},{6,4},{7,5},{8,10},{9,11},{10,... | collective-permute-start | bytes 196616 | tf_op jit(solution)/shard_map/ppermute | solution.py:192
  32.9 4.2 %collective-permute-start = (f32[128,128]{1,0:T(8,128)S(1)}, f32[128,128]{1,0:T(8,128)S(1)}, u32[]{:S(2)}, u32[]{:S(2)}) collective-permute-start(f32[128,128]{1,0:T(8,128)S(1)} %get-tuple-element.17.refs_0_), channel_id=1, source_target_pairs={{0,1},{1,0},{2,3},{3,2},{4,5},{5,4},{6,7},{7,6},{8,9},{9,8},{10,11... | collective-permute-start | bytes 196616 | tf_op jit(solution)/shard_map/ppermute | solution.py:192
  55.1 7.3 %collective-permute-start.5 = (f32[128,128]{1,0:T(8,128)S(1)}, f32[128,128]{1,0:T(8,128)S(1)}, u32[]{:S(2)}, u32[]{:S(2)}) collective-permute-start(f32[128,128]{1,0:T(8,128)S(1)} %get-tuple-element.20), channel_id=1, source_target_pairs={{0,3},{1,2},{2,1},{3,0},{4,7},{5,6},{6,5},{7,4},{8,11},{9,10},{10,... | collective-permute-start | bytes 196616 | tf_op jit(solution)/shard_map/ppermute | solution.py:192
  55.1 7.3 %collective-permute-start.4 = (f32[128,128]{1,0:T(8,128)S(1)}, f32[128,128]{1,0:T(8,128)S(1)}, u32[]{:S(2)}, u32[]{:S(2)}) collective-permute-start(f32[128,128]{1,0:T(8,128)S(1)} %get-tuple-element.20), channel_id=1, source_target_pairs={{0,2},{1,3},{2,0},{3,1},{4,6},{5,7},{6,4},{7,5},{8,10},{9,11},{10,... | collective-permute-start | bytes 196616 | tf_op jit(solution)/shard_map/ppermute | solution.py:192
  56.5 6.0 %collective-permute-start.3 = (f32[128,128]{1,0:T(8,128)S(1)}, f32[128,128]{1,0:T(8,128)S(1)}, u32[]{:S(2)}, u32[]{:S(2)}) collective-permute-start(f32[128,128]{1,0:T(8,128)S(1)} %get-tuple-element.20), channel_id=1, source_target_pairs={{0,1},{1,0},{2,3},{3,2},{4,5},{5,4},{6,7},{7,6},{8,9},{9,8},{10,11... | collective-permute-start | bytes 196616 | tf_op jit(solution)/shard_map/ppermute | solution.py:192

commit v2 on v0

v2 whole, which is shorter than its diff:
```python
import functools

import jax
import jax.numpy as jnp
from jax import lax
from jax.experimental import pallas as pl
from jax.experimental.pallas import tpu as pltpu
from jax.sharding import PartitionSpec as P

GROUP = 8
EXTRA = 8
CHUNK = 8
F32 = jnp.float32
BF16 = jnp.bfloat16

ascent_rate = 0.0015
select_cap = 0.5


def pieces(x):
    high = x.astype(BF16)
    rest = x - high.astype(F32)
    middle = rest.astype(BF16)
    low = (rest - middle.astype(F32)).astype(BF16)
    return high, middle, low


def pick(ones, x):
    width = x.shape[1]
    parts = jnp.dot(ones, jnp.concatenate(pieces(x), axis=1), preferred_element_type=F32)
    return parts[:, :width] + (parts[:, width : 2 * width] + parts[:, 2 * width :])


def inverse_of(x):
    guess = pltpu.reciprocal(x, approx=True)
    return guess * (2.0 - x * guess)


def hits_of(ids, test_rows):
    shape = (test_rows, ids.shape[1])
    return jnp.where(ids == lax.broadcasted_iota(jnp.int32, shape, 0).astype(F32), 1.0, 0.0).astype(BF16)


def columns_of(blocks, hits):
    return pick_rows(blocks.T, hits)


def pick_rows(x, ones):
    high, middle, low = [jnp.dot(piece, ones, preferred_element_type=F32) for piece in pieces(x)]
    return high + (middle + low)


def slot_pass(s, columns, tiles, ratios, logs):
    tile = tiles[s]
    left = 1.0 - columns[:, s : s + 1] * tile
    ratios[s] = tile * inverse_of(left)
    product = left[:8]
    for at in range(8, left.shape[0], 8):
        product = product * left[at : at + 8]
    logs[s : s + 1, :] = jnp.sum(jnp.log(product), axis=0, keepdims=True)


def first_kernel(limit, rows, cols, blocks, tiles, weights, payload, ratios, held, slot_weights, ids, mine, near, row_lanes, col_lanes, own, sems, tile_sem, weight_sem):
    slots, width = held.shape[0], held.shape[1]
    small = [
        pltpu.make_async_copy(source, target, sems.at[i])
        for i, (source, target) in enumerate(((cols, near), (cols, col_lanes), (rows, row_lanes), (blocks, own)))
    ]
    for copy in small:
        copy.start()
    tile_copies = []
    for group in range(slots // GROUP):
        part = pl.ds(group * GROUP, GROUP)
        tile_copies.append(pltpu.make_async_copy(tiles.at[part], held.at[part], tile_sem.at[group]))
        tile_copies[-1].start()
    small[0].wait()
    for s in range(slots):
        pltpu.make_async_copy(weights.at[pl.ds(near[0, s], 1)], slot_weights.at[pl.ds(s, 1)], weight_sem).start()
    for copy in small[1:]:
        copy.wait()
    live = lax.broadcasted_iota(jnp.int32, (1, slots), 1) < limit[0]
    lanes = jnp.where(live, col_lanes[...], -1).astype(F32)
    payload[slots:, :] = jnp.broadcast_to(jnp.concatenate([lanes] * (width // slots), axis=1), (EXTRA, width))
    mine[...] = jnp.broadcast_to(col_lanes[...].astype(F32), (width, slots)).T
    own_ids = row_lanes[...].astype(F32)
    ids[...] = jnp.broadcast_to(jnp.concatenate([own_ids] * (width // slots), axis=1), (EXTRA, width))
    columns = columns_of(own[...], hits_of(own_ids, own.shape[0]))
    for s in range(slots):
        if s % GROUP == 0:
            tile_copies[s // GROUP].wait()
        slot_pass(s, columns, held, ratios, payload)
    pltpu.make_async_copy(weights.at[pl.ds(0, slots)], slot_weights, weight_sem).wait()
    alive = lax.broadcasted_iota(jnp.int32, (slots, width), 0) < limit[0]
    slot_weights[...] = jnp.where(alive, slot_weights[...], 0.0)


def survive(gathered, others, mine, slot_weights):
    slots, width = slot_weights.shape
    here = mine[...]
    lanes = lax.broadcasted_iota(jnp.int32, (slots, width), 1)
    each = width // slots
    total = jnp.zeros((slots, width), F32)
    for start in range(0, gathered.shape[0], CHUNK):
        same = []
        for j in range(start, start + CHUNK, each):
            there = others[j, slots : slots + 1, :]
            for k in range(1, each):
                there = jnp.where(lanes < k * slots, there, others[j + k, slots : slots + 1, :])
            same.append(jnp.where(here == there, 1.0, 0.0).astype(BF16))
        rows = jnp.concatenate([gathered[j, :slots, :] for j in range(start, start + CHUNK)], axis=0)
        total = total + pick(jnp.concatenate(same, axis=1), rows)
    return slot_weights[...] * jnp.exp(total)


def slot_sums(survival, ratios, out):
    slots, width = survival.shape
    lanes = lax.broadcasted_iota(jnp.int32, (width, width), 1)
    ones = jnp.ones((width, width), BF16)
    total = jnp.zeros((width, width), F32)
    for s in range(slots):
        terms = ratios[s] * survival[s : s + 1, :]
        if s % 3 == 2:
            high = terms.astype(BF16)
            low = (terms - high.astype(F32)).astype(BF16)
            sums = jnp.dot(high, ones, preferred_element_type=F32) + jnp.dot(low, ones, preferred_element_type=F32)
        else:
            sums = jnp.sum(terms, axis=1, keepdims=True)
        total = jnp.where(lanes == s, sums, total)
    out[:slots, :] = total.T[:slots]


def gradient_kernel(gathered, mine, slot_weights, ratios, ids, out):
    slots = slot_weights.shape[0]
    slot_sums(survive(gathered, gathered, mine, slot_weights), ratios, out)
    out[slots:, :] = ids[...]


def last_gradient_kernel(gathered, others, mine, slot_weights, ratios, out, survival):
    survival[...] = survive(gathered, others, mine, slot_weights)
    slot_sums(survival[...], ratios, out)


def advance(current, gradient):
    rate = ascent_rate * gradient
    return current + (select_cap - current) * rate / (1.0 + rate)


def gradient_of(parts, ids, test_rows):
    slots = ids[0].shape[0] - EXTRA
    sums = [pick(hits_of(i[slots : slots + 1, :slots], test_rows), p[:slots, :]) for p, i in zip(parts, ids)]
    while len(sums) > 1:
        sums = [a + b for a, b in zip(sums[::2], sums[1::2])]
    return sums[0]


def next_kernel(blocks, held, *refs):
    *parts, current, logs, ratios = refs
    current[...] = advance(blocks[...], gradient_of(parts, parts, blocks.shape[0]))
    slots = held.shape[0]
    columns = columns_of(current[...], hits_of(parts[0][slots : slots + 1, :slots], blocks.shape[0]))
    for s in range(slots):
        slot_pass(s, columns, held, ratios, logs)


def tile_kernel(blocks, ids, survival, held, out, made, sems):
    slots = held.shape[0]
    columns = columns_of(blocks[...], hits_of(ids[:1, :slots], blocks.shape[0]))
    copies = []
    for s in range(slots):
        share = columns[:, s : s + 1]
        made[s] = survival[s : s + 1, :] * share * inverse_of(1.0 - share * held[s])
        if s % GROUP == GROUP - 1:
            part = pl.ds(s + 1 - GROUP, GROUP)
            copies.append(pltpu.make_async_copy(made.at[part], out.at[part], sems.at[s // GROUP]))
            copies[-1].start()
    for copy in copies:
        copy.wait()


def last_kernel(branches, current, *refs):
    *given, gradient, following = refs
    total = gradient_of(given[:branches], given[branches:], current.shape[0])
    gradient[...] = total
    following[...] = advance(current[...], total)


SMEM = pl.BlockSpec(memory_space=pltpu.SMEM)
VMEM = pl.BlockSpec(memory_space=pltpu.VMEM)
HBM = pl.BlockSpec(memory_space=pltpu.HBM)
PARAMS = pltpu.CompilerParams(vmem_limit_bytes=24 << 20)


def body(tests, branches, select, tiles, row_block, col_block, counts, weights):
    slots, width = tiles.shape[0], tiles.shape[1]
    blocks = select.reshape(-1, width)
    weight_rows = weights.reshape(-1, width)
    full = jax.ShapeDtypeStruct(tiles.shape, F32)
    per_slot = jax.ShapeDtypeStruct((slots, width), F32)
    labelled = jax.ShapeDtypeStruct((slots + EXTRA, width), F32)
    label = jax.ShapeDtypeStruct((EXTRA, width), F32)
    per_test = jax.ShapeDtypeStruct(blocks.shape, F32)
    lanes = pltpu.VMEM((1, slots), jnp.int32)
    dma = pltpu.SemaphoreType.DMA

    def call(kernel, outs, ins, name, **more):
        return pl.pallas_call(
            kernel,
            out_shape=outs,
            in_specs=more.pop("in_specs", [VMEM] * len(ins)),
            out_specs=more.pop("out_specs", jax.tree.map(lambda _: VMEM, outs)),
            compiler_params=PARAMS,
            name=name,
            **more,
        )(*ins)

    def over_tests(x):
        return lax.all_to_all(jnp.broadcast_to(x[None], (tests,) + x.shape), "tests", 0, 0)

    def over_branches(x):
        return [x] + [lax.ppermute(x, "branches", [(b, b ^ k) for b in range(branches)]) for k in range(1, branches)]

    payload, ratios, held, slot_weights, ids, mine = call(
        first_kernel,
        (labelled, full, full, per_slot, label, per_slot),
        (counts, row_block.reshape(1, -1), col_block.reshape(1, -1), blocks, tiles, weight_rows),
        "first_logs",
        in_specs=[SMEM] + [HBM] * 5,
        scratch_shapes=[
            pltpu.SMEM((1, slots), jnp.int32),
            lanes,
            lanes,
            pltpu.VMEM(blocks.shape, F32),
            dma((4,)),
            dma((slots // GROUP,)),
            dma,
        ],
    )
    others = over_tests(payload)
    parts = over_branches(call(gradient_kernel, labelled, (others, mine, slot_weights, ratios, ids), "gradient"))
    current, logs, ratios = call(next_kernel, (per_test, per_slot, full), (blocks, held, *parts), "next_logs")
    sums, survival = call(
        last_gradient_kernel, (per_slot, per_slot), (over_tests(logs), others, mine, slot_weights, ratios), "last_gradient"
    )
    last_parts = over_branches(sums)
    tile_grads = call(
        tile_kernel,
        full,
        (current, ids, survival, held),
        "tile_gradients",
        out_specs=HBM,
        scratch_shapes=[pltpu.VMEM(tiles.shape, F32), dma((slots // GROUP,))],
    )
    gradient, following = call(
        functools.partial(last_kernel, branches), (per_test, per_test), (current, *last_parts, *parts), "last_update"
    )
    return gradient.reshape(-1), tile_grads, following.reshape(-1)


def solution(mesh):
    return jax.shard_map(
        functools.partial(body, mesh.shape["tests"], mesh.shape["branches"]),
        mesh=mesh,
        in_specs=(
            P("tests"),
            P(("tests", "branches"), None, None),
            P(("tests", "branches")),
            P(("tests", "branches")),
            P(("tests", "branches")),
            P("branches"),
        ),
        out_specs=(P("tests"), P(("tests", "branches"), None, None), P("tests")),
        check_vma=False,
    )
```

time: 271 us -> 54.2 us (0.20)
  waiting for transfers between devices: 221 us -> 2.32 us
  other arithmetic: 30.2 us -> 0 us
  blocking collectives: 0 us -> 30 us
  between operations: 14.6 us -> 1.37 us
  Pallas kernels: 0 us -> 10.8 us
  starting transfers between devices: 0.16 us -> 3.79 us
    psum x4 -> x0, waiting for transfers between devices: 221 us -> none  [the longest x2 159 us: body(): summed = lax.psum(partial_value, 'tests')]
    all_to_all x0 -> x2, blocking collectives: none -> 30 us  [over_tests(): lax.all_to_all(jnp.broadcast_to(x[None], (tests,) + x.shape), 'tests', 0, 0)]
    reduce_sum x3 -> x0, other arithmetic: 11.2 us -> none  [the longest x2 6.68 us: tile_logs(): logs = jnp.sum(jnp.log1p(-picked[:, :, None] * tiles), axis=1)]
    pallas_call x0 -> x6, Pallas kernels: none -> 10.8 us  [call(): pl.pallas_call(kernel, out_shape=outs, in_specs=more.pop('in_specs', [VME...]
    select_n x3 -> x0, other arithmetic: 7.2 us -> none  [the longest x1 5.88 us: tile_terms(): jnp.where(live[:, None, None], tile_part, jnp.zeros_like(tile_part))]
    scatter-add x4 -> x0, other arithmetic: 6.65 us -> none  [the longest x2 3.73 us: body(): jnp.zeros((branch_rows, width), jnp.float32).at[col_block].add(slot_logs)]
    unnamed x7 -> x10, local copies, waits for them, and re-layouts: 1.49 us -> 5.55 us
    ppermute x0 -> x6, starting transfers between devices: none -> 3.79 us  [over_branches(): lax.ppermute(x, 'branches', [(b, b ^ k) for b in range(branches)])]
  transfers between devices with their start and end apart: 4 -> 6, of which waited for: 4 -> 2; matrix products, arithmetic and copies ran while one was open for 0% -> 0% of each run, Pallas kernels for 0% -> 5%
where the time goes in v2:
time: 54.2 us; the launch traced here: 53.9 us
  blocking collectives  30 us (55%)
  Pallas kernels  10.8 us (20%)
  local copies, waits for them, and re-layouts  5.59 us (10%)
  starting transfers between devices  3.79 us (7%)
  waiting for transfers between devices  2.32 us (4%)
  between operations  1.37 us (3%)
    all_to_all x2, blocking collectives, over_tests(): lax.all_to_all(jnp.broadcast_to(x[None], (tests,) + x.shape), 'tests', 0, 0)  30 us
    pallas_call x6, Pallas kernels, call(): pl.pallas_call(kernel, out_shape=outs, in_specs=more.pop('in_specs', [VME...  10.8 us
    unnamed x10, local copies, waits for them, and re-layouts  5.55 us
    ppermute x6, starting transfers between devices, over_branches(): lax.ppermute(x, 'branches', [(b, b ^ k) for b in range(branches)])  3.79 us
    ppermute x6, waiting for transfers between devices, over_branches(): lax.ppermute(x, 'branches', [(b, b ^ k) for b in range(branches)])  2.32 us
  transfers between devices with their start and end apart: 6, of which 2 were waited for; matrix products, arithmetic and copies ran while one was open for 0% of the time, Pallas kernels for 5%

profile of v2, /device:TPU:0, one launch (start us, length us, event | category | flops | bytes accessed | tf_op | source)
XLA Modules:
  0.0 53.9 jit_solution(16834536295358069819)
XLA Ops:
  1.3 0.0 copy-start
  1.3 2.2 %copy-done = f32[64,128,128]{2,1,0:T(8,128)S(1)} copy-done((f32[64,128,128]{2,1,0:T(8,128)S(1)}, f32[64,128,128]{2,1,0:T(8,128)}, u32[]{:S(2)}) %copy-start) | copy-done | bytes 4194328
  3.5 0.0 copy-start.1
  3.5 1.2 %copy-done.1 = f32[262144]{0:T(1024)S(1)} copy-done((f32[262144]{0:T(1024)S(1)}, f32[262144]{0:T(1024)}, u32[]{:S(2)}) %copy-start.1) | copy-done | bytes 1048600
  4.7 0.0 copy-start.2
  4.7 0.8 %copy-done.2 = f32[16384]{0:T(1024)S(1)} copy-done((f32[16384]{0:T(1024)S(1)}, f32[16384]{0:T(1024)}, u32[]{:S(2)}) %copy-start.2) | copy-done | bytes 65560
  5.5 0.0 copy-start.3
  5.5 0.7 %copy-done.3 = s32[64]{0:T(128)S(1)} copy-done((s32[64]{0:T(128)S(1)}, s32[64]{0:T(128)}, u32[]{:S(2)}) %copy-start.3) | copy-done | bytes 280
  6.2 0.0 copy-start.4
  6.2 0.7 %copy-done.4 = s32[64]{0:T(128)S(1)} copy-done((s32[64]{0:T(128)S(1)}, s32[64]{0:T(128)}, u32[]{:S(2)}) %copy-start.4) | copy-done | bytes 280
  6.8 3.0 %first_logs.1 = (f32[72,128]{1,0:T(8,128)S(1)}, f32[64,128,128]{2,1,0:T(8,128)S(1)}, f32[64,128,128]{2,1,0:T(8,128)S(1)}, f32[64,128]{1,0:T(8,128)S(1)}, f32[8,128]{1,0:T(8,128)S(1)}, /*index=5*/f32[64,128]{1,0:T(8,128)S(1)}) custom-call(s32[1]{0:T(128)S(6)} %copy.9.limit, s32[1,64]{1,0:T(1,128)S(1)} %bitcast.9, s32[1,64]{1,0:T(1,128)S(1)} %bitcast.10, ...), custom_call_target="tpu_custom_call" | custom-call | tf_op jit(solution)/shard_map/first_logs/pallas_call | solution.py:206
  9.9 17.4 %all_to_all.10.gathered.others = f32[8,72,128]{2,1,0:T(8,128)S(1)} all-to-all(f32[8,72,128]{2,1,0:T(8,128)S(1)} %broadcast_in_dim.4), channel_id=1, replica_groups=mesh['tests'=8,'branches'=4] {'tests'}, dimensions={0} | all-to-all | bytes 589824 | tf_op jit(solution)/shard_map/all_to_all | solution.py:217
  27.3 1.1 %gradient.1.refs_0_.refs_4_ = f32[72,128]{1,0:T(8,128)S(1)} custom-call(f32[8,72,128]{2,1,0:T(8,128)S(1)} %all_to_all.10.gathered.others, f32[64,128]{1,0:T(8,128)S(1)} %get-tuple-element.18.mine, f32[64,128]{1,0:T(8,128)S(1)} %get-tuple-element.19.slot_weights, f32[64,128,128]{2,1,0:T(8,128)S(1)} %get-tuple-element.20.ratios, ...), custom_call_target="tpu_custom_call" | custom-call | tf_op jit(solution)/shard_map/gradient/pallas_call | solution.py:206
  28.5 0.0 collective-permute-start.2
  28.5 1.6 %collective-permute-start.1 = (f32[72,128]{1,0:T(8,128)S(1)}, f32[72,128]{1,0:T(8,128)S(1)}, u32[]{:S(2)}, u32[]{:S(2)}) collective-permute-start(f32[72,128]{1,0:T(8,128)S(1)} %gradient.1.refs_0_.refs_4_), channel_id=1, source_target_pairs={{0,2},{1,3},{2,0},{3,1},{4,6},{5,7},{6,4},{7,5},{8,10},{9,11},{10,... | collective-permute-start | bytes 110600 | tf_op jit(solution)/shard_map/ppermute | solution.py:220
  30.1 0.3 collective-permute-start
  30.4 1.8 %collective-permute-done.2.refs_3_.refs_7_ = f32[72,128]{1,0:T(8,128)S(1)} collective-permute-done((f32[72,128]{1,0:T(8,128)S(1)}, f32[72,128]{1,0:T(8,128)S(1)}, u32[]{:S(2)}, u32[]{:S(2)}) %collective-permute-start.2) | collective-permute-done | bytes 36896 | tf_op jit(solution)/shard_map/ppermute | solution.py:220
  32.2 0.5 collective-permute-done.1.refs_2_.refs_6_
  32.7 0.0 collective-permute-done.refs_1_.refs_5_
  32.7 1.9 %next_logs.1 = (f32[128,128]{1,0:T(8,128)S(1)}, f32[64,128]{1,0:T(8,128)S(1)}, f32[64,128,128]{2,1,0:T(8,128)S(1)}) custom-call(f32[128,128]{1,0:T(8,128)S(1)} %bitcast.8, f32[64,128,128]{2,1,0:T(8,128)S(1)} %get-tuple-element.16.held, f32[72,128]{1,0:T(8,128)S(1)} %gradient.1.refs_0_.refs_4_, f32[72,128]{1,0:T(8,128)S(1)} %collective-permute-done.refs_1_.refs_5_, ...), custom_call_target="tpu_custom_call" | custom-call | tf_op jit(solution)/shard_map/next_logs/pallas_call | solution.py:206
  34.7 12.6 %all_to_all.11.gathered = f32[8,64,128]{2,1,0:T(8,128)S(1)} all-to-all(f32[8,64,128]{2,1,0:T(8,128)S(1)} %broadcast_in_dim.5), channel_id=1, replica_groups=mesh['tests'=8,'branches'=4] {'tests'}, dimensions={0} | all-to-all | bytes 524288 | tf_op jit(solution)/shard_map/all_to_all | solution.py:217
  47.2 1.1 %last_gradient.1 = (f32[64,128]{1,0:T(8,128)S(1)}, f32[64,128]{1,0:T(8,128)S(1)}) custom-call(f32[8,64,128]{2,1,0:T(8,128)S(1)} %all_to_all.11.gathered, f32[8,72,128]{2,1,0:T(8,128)S(1)} %all_to_all.10.gathered.others, f32[64,128]{1,0:T(8,128)S(1)} %get-tuple-element.18.mine, f32[64,128]{1,0:T(8,128)S(1)} %get-tuple-element.19.slot_weights, ...), custom_call_target="tpu_custom_call" | custom-call | tf_op jit(solution)/shard_map/last_gradient/pallas_call | solution.py:206
  48.4 0.0 collective-permute-start.5
  48.4 1.1 %collective-permute-start.4 = (f32[64,128]{1,0:T(8,128)S(1)}, f32[64,128]{1,0:T(8,128)S(1)}, u32[]{:S(2)}, u32[]{:S(2)}) collective-permute-start(f32[64,128]{1,0:T(8,128)S(1)} %get-tuple-element.25.refs_0_), channel_id=1, source_target_pairs={{0,2},{1,3},{2,0},{3,1},{4,6},{5,7},{6,4},{7,5},{8,10},{9,11},{10,... | collective-permute-start | bytes 98312 | tf_op jit(solution)/shard_map/ppermute | solution.py:220
  49.5 0.8 %collective-permute-start.3 = (f32[64,128]{1,0:T(8,128)S(1)}, f32[64,128]{1,0:T(8,128)S(1)}, u32[]{:S(2)}, u32[]{:S(2)}) collective-permute-start(f32[64,128]{1,0:T(8,128)S(1)} %get-tuple-element.25.refs_0_), channel_id=1, source_target_pairs={{0,1},{1,0},{2,3},{3,2},{4,5},{5,4},{6,7},{7,6},{8,9},{9,8},{10,11... | collective-permute-start | bytes 98312 | tf_op jit(solution)/shard_map/ppermute | solution.py:220
  50.3 2.7 %tile_gradients.1 = f32[64,128,128]{2,1,0:T(8,128)} custom-call(f32[128,128]{1,0:T(8,128)S(1)} %get-tuple-element.22.current.blocks, f32[8,128]{1,0:T(8,128)S(1)} %get-tuple-element.21.ids, f32[64,128]{1,0:T(8,128)S(1)} %get-tuple-element.27.survival, f32[64,128,128]{2,1,0:T(8,128)S(1)} %get-tuple-element.16.held), custom_call_target="tpu_custom_call" | custom-call | tf_op jit(solution)/shard_map/tile_gradients/pallas_call | solution.py:206
  53.0 0.0 collective-permute-done.5.refs_3_
  53.0 0.0 collective-permute-done.4.refs_2_
  53.0 0.0 collective-permute-done.3.refs_1_
  53.0 0.9 %last_update.1 = (f32[128,128]{1,0:T(8,128)}, f32[128,128]{1,0:T(8,128)}) custom-call(f32[128,128]{1,0:T(8,128)S(1)} %get-tuple-element.22.current.blocks, f32[64,128]{1,0:T(8,128)S(1)} %get-tuple-element.25.refs_0_, f32[64,128]{1,0:T(8,128)S(1)} %collective-permute-done.3.refs_1_, f32[64,128]{1,0:T(8,128)S(1)} %collective-permute-done.4.refs_2_, ...), custom_call_target="tpu_custom_call" | custom-call | tf_op jit(solution)/shard_map/last_update/pallas_call | solution.py:206
  (2 shorter events, 0.0 us)
Async XLA Ops:
  1.3 2.2 %copy-start = (f32[64,128,128]{2,1,0:T(8,128)S(1)}, f32[64,128,128]{2,1,0:T(8,128)}, u32[]{:S(2)}) copy-start(f32[64,128,128]{2,1,0:T(8,128)} %tiles.1) | copy-start | bytes 12582916
  3.5 1.2 %copy-start.1 = (f32[262144]{0:T(1024)S(1)}, f32[262144]{0:T(1024)}, u32[]{:S(2)}) copy-start(f32[262144]{0:T(1024)} %param.11) | copy-start | bytes 3145732
  4.7 0.8 %copy-start.2 = (f32[16384]{0:T(1024)S(1)}, f32[16384]{0:T(1024)}, u32[]{:S(2)}) copy-start(f32[16384]{0:T(1024)} %param.6) | copy-start | bytes 196612
  5.5 0.7 %copy-start.3 = (s32[64]{0:T(128)S(1)}, s32[64]{0:T(128)}, u32[]{:S(2)}) copy-start(s32[64]{0:T(128)} %param.8) | copy-start | bytes 772
  6.2 0.7 %copy-start.4 = (s32[64]{0:T(128)S(1)}, s32[64]{0:T(128)}, u32[]{:S(2)}) copy-start(s32[64]{0:T(128)} %param.9) | copy-start | bytes 772
  28.5 3.7 %collective-permute-start.2 = (f32[72,128]{1,0:T(8,128)S(1)}, f32[72,128]{1,0:T(8,128)S(1)}, u32[]{:S(2)}, u32[]{:S(2)}) collective-permute-start(f32[72,128]{1,0:T(8,128)S(1)} %gradient.1.refs_0_.refs_4_), channel_id=1, source_target_pairs={{0,3},{1,2},{2,1},{3,0},{4,7},{5,6},{6,5},{7,4},{8,11},{9,10},{10,... | collective-permute-start | bytes 110600 | tf_op jit(solution)/shard_map/ppermute | solution.py:220
  28.5 4.2 %collective-permute-start.1 = (f32[72,128]{1,0:T(8,128)S(1)}, f32[72,128]{1,0:T(8,128)S(1)}, u32[]{:S(2)}, u32[]{:S(2)}) collective-permute-start(f32[72,128]{1,0:T(8,128)S(1)} %gradient.1.refs_0_.refs_4_), channel_id=1, source_target_pairs={{0,2},{1,3},{2,0},{3,1},{4,6},{5,7},{6,4},{7,5},{8,10},{9,11},{10,... | collective-permute-start | bytes 110600 | tf_op jit(solution)/shard_map/ppermute | solution.py:220
  30.1 2.6 %collective-permute-start = (f32[72,128]{1,0:T(8,128)S(1)}, f32[72,128]{1,0:T(8,128)S(1)}, u32[]{:S(2)}, u32[]{:S(2)}) collective-permute-start(f32[72,128]{1,0:T(8,128)S(1)} %gradient.1.refs_0_.refs_4_), channel_id=1, source_target_pairs={{0,1},{1,0},{2,3},{3,2},{4,5},{5,4},{6,7},{7,6},{8,9},{9,8},{10,11... | collective-permute-start | bytes 110600 | tf_op jit(solution)/shard_map/ppermute | solution.py:220
  48.4 4.6 %collective-permute-start.5 = (f32[64,128]{1,0:T(8,128)S(1)}, f32[64,128]{1,0:T(8,128)S(1)}, u32[]{:S(2)}, u32[]{:S(2)}) collective-permute-start(f32[64,128]{1,0:T(8,128)S(1)} %get-tuple-element.25.refs_0_), channel_id=1, source_target_pairs={{0,3},{1,2},{2,1},{3,0},{4,7},{5,6},{6,5},{7,4},{8,11},{9,10},{10,... | collective-permute-start | bytes 98312 | tf_op jit(solution)/shard_map/ppermute | solution.py:220
  48.4 4.6 %collective-permute-start.4 = (f32[64,128]{1,0:T(8,128)S(1)}, f32[64,128]{1,0:T(8,128)S(1)}, u32[]{:S(2)}, u32[]{:S(2)}) collective-permute-start(f32[64,128]{1,0:T(8,128)S(1)} %get-tuple-element.25.refs_0_), channel_id=1, source_target_pairs={{0,2},{1,3},{2,0},{3,1},{4,6},{5,7},{6,4},{7,5},{8,10},{9,11},{10,... | collective-permute-start | bytes 98312 | tf_op jit(solution)/shard_map/ppermute | solution.py:220
  49.5 3.5 %collective-permute-start.3 = (f32[64,128]{1,0:T(8,128)S(1)}, f32[64,128]{1,0:T(8,128)S(1)}, u32[]{:S(2)}, u32[]{:S(2)}) collective-permute-start(f32[64,128]{1,0:T(8,128)S(1)} %get-tuple-element.25.refs_0_), channel_id=1, source_target_pairs={{0,1},{1,0},{2,3},{3,2},{4,5},{5,4},{6,7},{7,6},{8,9},{9,8},{10,11... | collective-permute-start | bytes 98312 | tf_op jit(solution)/shard_map/ppermute | solution.py:220

commit v3 on v2

--- a/solution.py
+++ b/solution.py
@@ -10,6 +10,9 @@
 GROUP = 8
 EXTRA = 8
 CHUNK = 8
+FEW = 16
+HALVES = 2
+SHARED = 3
 F32 = jnp.float32
 BF16 = jnp.bfloat16
 
@@ -32,8 +35,7 @@
 
 
 def inverse_of(x):
-    guess = pltpu.reciprocal(x, approx=True)
-    return guess * (2.0 - x * guess)
+    return pltpu.reciprocal(x, approx=True)
 
 
 def hits_of(ids, test_rows):
@@ -42,25 +44,52 @@
 
 
 def columns_of(blocks, hits):
-    return pick_rows(blocks.T, hits)
-
-
-def pick_rows(x, ones):
-    high, middle, low = [jnp.dot(piece, ones, preferred_element_type=F32) for piece in pieces(x)]
+    return [jnp.dot(piece, hits, preferred_element_type=F32) for piece in pieces(blocks.T)]
+
+
+def total_of(columns):
+    high, middle, low = columns
     return high + (middle + low)
 
 
-def slot_pass(s, columns, tiles, ratios, logs):
-    tile = tiles[s]
-    left = 1.0 - columns[:, s : s + 1] * tile
-    ratios[s] = tile * inverse_of(left)
-    product = left[:8]
-    for at in range(8, left.shape[0], 8):
-        product = product * left[at : at + 8]
-    logs[s : s + 1, :] = jnp.sum(jnp.log(product), axis=0, keepdims=True)
-
-
-def first_kernel(limit, rows, cols, blocks, tiles, weights, payload, ratios, held, slot_weights, ids, mine, near, row_lanes, col_lanes, own, sems, tile_sem, weight_sem):
+def spread_columns(columns):
+    width, slots = columns[0].shape
+    whole = total_of(columns)
+    stack = jnp.concatenate(columns, axis=1).astype(BF16)
+    shape = (len(columns) * slots, 2 * width)
+    slot = lax.broadcasted_iota(jnp.int32, shape, 0) % slots - lax.broadcasted_iota(jnp.int32, shape, 1) // width
+    for s in range(0, slots, 2):
+        if (s // 2) % SHARED == SHARED - 1:
+            both = jnp.dot(stack, jnp.where(slot == s, 1.0, 0.0).astype(BF16), preferred_element_type=F32)
+            yield both[:, :width]
+            yield both[:, width:]
+        else:
+            yield whole[:, s : s + 1]
+            yield whole[:, s + 1 : s + 2]
+
+
+def slots_pass(columns, tiles, ratios, products, before=lambda s: None):
+    for s, column in enumerate(spread_columns(columns)):
+        before(s)
+        tile = tiles[s]
+        left = 1.0 - column * tile
+        ratios[s] = tile * inverse_of(left)
+        product = left[:8]
+        for at in range(8, left.shape[0], 8):
+            product = product * left[at : at + 8]
+        products[8 * s : 8 * s + 8, :] = product
+
+
+def logs_of(products):
+    slots = products.shape[0] // 8
+    part = lambda k: products[pl.ds(k, slots, stride=8), :]
+    total = jnp.log(part(0) * part(1))
+    for k in range(2, 8, 2):
+        total = total + jnp.log(part(k) * part(k + 1))
+    return total
+
+
+def first_kernel(limit, rows, cols, blocks, tiles, weights, payload, ratios, held, slot_weights, ids, mine, near, row_lanes, col_lanes, own, products, sems, tile_sem, weight_sem):
     slots, width = held.shape[0], held.shape[1]
     small = [
         pltpu.make_async_copy(source, target, sems.at[i])
@@ -69,8 +98,9 @@
     for copy in small:
         copy.start()
     tile_copies = []
-    for group in range(slots // GROUP):
-        part = pl.ds(group * GROUP, GROUP)
+    chunk = slots // HALVES
+    for group in range(HALVES):
+        part = pl.ds(group * chunk, chunk)
         tile_copies.append(pltpu.make_async_copy(tiles.at[part], held.at[part], tile_sem.at[group]))
         tile_copies[-1].start()
     small[0].wait()
@@ -81,35 +111,103 @@
     live = lax.broadcasted_iota(jnp.int32, (1, slots), 1) < limit[0]
     lanes = jnp.where(live, col_lanes[...], -1).astype(F32)
     payload[slots:, :] = jnp.broadcast_to(jnp.concatenate([lanes] * (width // slots), axis=1), (EXTRA, width))
-    mine[...] = jnp.broadcast_to(col_lanes[...].astype(F32), (width, slots)).T
+    mine[...] = jnp.broadcast_to(jnp.where(live, col_lanes[...], -2).astype(F32), (width, slots)).T
     own_ids = row_lanes[...].astype(F32)
     ids[...] = jnp.broadcast_to(jnp.concatenate([own_ids] * (width // slots), axis=1), (EXTRA, width))
     columns = columns_of(own[...], hits_of(own_ids, own.shape[0]))
-    for s in range(slots):
-        if s % GROUP == 0:
-            tile_copies[s // GROUP].wait()
-        slot_pass(s, columns, held, ratios, payload)
+
+    def arrive(s):
+        if s % chunk == 0:
+            tile_copies[s // chunk].wait()
+
+    slots_pass(columns, held, ratios, products, arrive)
+    payload[:slots, :] = logs_of(products)
     pltpu.make_async_copy(weights.at[pl.ds(0, slots)], slot_weights, weight_sem).wait()
     alive = lax.broadcasted_iota(jnp.int32, (slots, width), 0) < limit[0]
     slot_weights[...] = jnp.where(alive, slot_weights[...], 0.0)
 
 
-def survive(gathered, others, mine, slot_weights):
-    slots, width = slot_weights.shape
+def matches(others, mine, start):
+    slots, width = mine.shape
     here = mine[...]
     lanes = lax.broadcasted_iota(jnp.int32, (slots, width), 1)
     each = width // slots
+    same = []
+    for j in range(start, start + CHUNK, each):
+        there = others[j, slots : slots + 1, :]
+        for k in range(1, each):
+            there = jnp.where(lanes < k * slots, there, others[j + k, slots : slots + 1, :])
+        same.append(jnp.where(here == there, 1.0, 0.0))
+    return jnp.concatenate(same, axis=1)
+
+
+def log_survival(gathered, others, mine):
+    slots, width = mine.shape
     total = jnp.zeros((slots, width), F32)
     for start in range(0, gathered.shape[0], CHUNK):
-        same = []
-        for j in range(start, start + CHUNK, each):
-            there = others[j, slots : slots + 1, :]
-            for k in range(1, each):
-                there = jnp.where(lanes < k * slots, there, others[j + k, slots : slots + 1, :])
-            same.append(jnp.where(here == there, 1.0, 0.0).astype(BF16))
         rows = jnp.concatenate([gathered[j, :slots, :] for j in range(start, start + CHUNK)], axis=0)
-        total = total + pick(jnp.concatenate(same, axis=1), rows)
-    return slot_weights[...] * jnp.exp(total)
+        total = total + pick(matches(others, mine, start).astype(BF16), rows)
+    return total
+
+
+def all_rows_kernel(gathered, others, mine, out):
+    out[...] = log_survival(gathered, others, mine)
+
+
+def few_rows_kernel(received, places, own, logs, out):
+    others = pick(places[...].astype(BF16), received[...].reshape(-1, received.shape[-1]))
+    out[...] = others + pick(own[...].astype(BF16), logs[...])
+
+
+def before_in(shape, slots):
+    k, l = [lax.broadcasted_iota(jnp.int32, shape, d) for d in (0, 1)]
+    return jnp.where((k // slots == l // slots) & (k < l), 1.0, 0.0).astype(BF16)
+
+
+def plan_kernel(others, mine, payload, after, few, sent, places, own):
+    del after
+    slots, width = mine.shape
+    tests = others.shape[0]
+    every = tests * slots
+    same = matches(others, mine, 0)
+    owner = lax.broadcasted_iota(jnp.int32, (every, width), 0) // slots
+    owners = jnp.where(owner == lax.broadcasted_iota(jnp.int32, (every, width), 1), 1.0, 0.0).astype(BF16)
+
+    wanted = jnp.broadcast_to(jnp.max(same, axis=0, keepdims=True), (8, every))
+    order = before_in((width, width), slots)
+    ranks = jnp.concatenate(
+        [jnp.dot(wanted[:, at : at + width].astype(BF16), order, preferred_element_type=F32) for at in range(0, every, width)],
+        axis=1,
+    )
+    shape = (tests * FEW, every)
+    place = lax.broadcasted_iota(jnp.int32, shape, 0)
+    source = place // FEW
+    here = (source == lax.broadcasted_iota(jnp.int32, shape, 1) // slots) & (source != lax.axis_index("tests")) & (wanted[:1] > 0.0)
+    into = jnp.where(here & (ranks[:1] == (place % FEW).astype(F32)), 1.0, 0.0).astype(BF16)
+    places[...] = lax.dot_general(same.astype(BF16), into, (((1,), (1,)), ((), ())), preferred_element_type=F32)
+    own[...] = jnp.where(mine[...][:, :slots] == payload[slots : slots + 1, :slots], 1.0, 0.0)
+
+    asked = jnp.dot(same.astype(BF16), owners, preferred_element_type=F32).T[:tests]
+    asked = jnp.where(asked > 0.0, 1.0, 0.0)
+    ranks = jnp.dot(asked.astype(BF16), before_in((slots, slots), slots), preferred_element_type=F32)
+    row = lax.broadcasted_iota(jnp.int32, (FEW, slots), 0).astype(F32)
+    sent[...] = jnp.concatenate(
+        [jnp.where((asked[j : j + 1] > 0.0) & (ranks[j : j + 1] == row), 1.0, 0.0) for j in range(tests)], axis=0
+    )
+
+    table = jnp.concatenate([others[j, slots : slots + 1, :] for j in range(tests)], axis=0)
+    there = [table[j : j + 1, :slots] for j in range(tests)]
+    there = jnp.concatenate(there, axis=1)
+    down = jnp.broadcast_to(table[:, None, :], (tests, width // tests, width)).reshape(width, width).T[:slots]
+    lane = lax.broadcasted_iota(jnp.int32, (1, width), 1)
+    most = jnp.zeros((1, width), F32)
+    for i in range(tests):
+        at = i * (width // tests)
+        column = jnp.where(down[:, at : at + 1] < 0.0, -2.0, down[:, at : at + 1])
+        met = jnp.where(column == there, 1.0, 0.0).astype(BF16)
+        counts = jnp.sum(jnp.where(jnp.dot(met, owners, preferred_element_type=F32) > 0.0, 1.0, 0.0), axis=0, keepdims=True)
+        most = jnp.maximum(most, jnp.where(lane == i, 0.0, counts))
+    few[...] = jnp.broadcast_to(jnp.where(jnp.max(most, axis=1, keepdims=True) <= FEW, 1.0, 0.0), few.shape)
 
 
 def slot_sums(survival, ratios, out):
@@ -131,13 +229,14 @@
 
 def gradient_kernel(gathered, mine, slot_weights, ratios, ids, out):
     slots = slot_weights.shape[0]
-    slot_sums(survive(gathered, gathered, mine, slot_weights), ratios, out)
+    slot_sums(slot_weights[...] * jnp.exp(log_survival(gathered, gathered, mine)), ratios, out)
     out[slots:, :] = ids[...]
 
 
-def last_gradient_kernel(gathered, others, mine, slot_weights, ratios, out, survival):
-    survival[...] = survive(gathered, others, mine, slot_weights)
+def last_gradient_kernel(total, slot_weights, ratios, few, out, survival):
+    survival[...] = slot_weights[...] * jnp.exp(total[...])
     slot_sums(survival[...], ratios, out)
+    out[slot_weights.shape[0] :, :] = few[...]
 
 
 def advance(current, gradient):
@@ -153,18 +252,22 @@
     return sums[0]
 
 
-def next_kernel(blocks, held, *refs):
-    *parts, current, logs, ratios = refs
-    current[...] = advance(blocks[...], gradient_of(parts, parts, blocks.shape[0]))
-    slots = held.shape[0]
-    columns = columns_of(current[...], hits_of(parts[0][slots : slots + 1, :slots], blocks.shape[0]))
-    for s in range(slots):
-        slot_pass(s, columns, held, ratios, logs)
+def next_kernel(branches, blocks, held, *refs):
+    parts, refs = refs[:branches], refs[branches:]
+    *sent, current, logs, ratios, out, products = refs if len(refs) == 6 else (*refs[:3], None, refs[3])
+    test_rows, slots = blocks.shape[0], held.shape[0]
+    current[...] = advance(blocks[...], gradient_of(parts, parts, test_rows))
+    columns = columns_of(current[...], hits_of(parts[0][slots : slots + 1, :slots], test_rows))
+    slots_pass(columns, held, ratios, products)
+    rows = logs_of(products)
+    logs[...] = rows
+    if sent:
+        out[...] = pick(sent[0][...].astype(BF16), rows).reshape(out.shape)
 
 
 def tile_kernel(blocks, ids, survival, held, out, made, sems):
     slots = held.shape[0]
-    columns = columns_of(blocks[...], hits_of(ids[:1, :slots], blocks.shape[0]))
+    columns = total_of(columns_of(blocks[...], hits_of(ids[:1, :slots], blocks.shape[0])))
     copies = []
     for s in range(slots):
         share = columns[:, s : s + 1]
@@ -178,10 +281,14 @@
 
 
 def last_kernel(branches, current, *refs):
-    *given, gradient, following = refs
-    total = gradient_of(given[:branches], given[branches:], current.shape[0])
+    *given, gradient, following, few = refs
+    parts, ids = given[:branches], given[branches:]
+    total = gradient_of(parts, ids, current.shape[0])
     gradient[...] = total
     following[...] = advance(current[...], total)
+    slots = parts[0].shape[0] - EXTRA
+    fewest = functools.reduce(jnp.minimum, [p[slots : slots + 1, :] for p in parts])
+    few[0] = jnp.min(fewest).astype(jnp.int32)
 
 
 SMEM = pl.BlockSpec(memory_space=pltpu.SMEM)
@@ -190,7 +297,7 @@
 PARAMS = pltpu.CompilerParams(vmem_limit_bytes=24 << 20)
 
 
-def body(tests, branches, select, tiles, row_block, col_block, counts, weights):
+def sweep(tests, branches, few_rows, select, tiles, row_block, col_block, counts, weights):
     slots, width = tiles.shape[0], tiles.shape[1]
     blocks = select.reshape(-1, width)
     weight_rows = weights.reshape(-1, width)
@@ -200,7 +307,9 @@
     label = jax.ShapeDtypeStruct((EXTRA, width), F32)
     per_test = jax.ShapeDtypeStruct(blocks.shape, F32)
     lanes = pltpu.VMEM((1, slots), jnp.int32)
+    products = pltpu.VMEM((8 * slots, width), F32)
     dma = pltpu.SemaphoreType.DMA
+    far = lambda x: pltpu.with_memory_space_constraint(x, pltpu.HBM)
 
     def call(kernel, outs, ins, name, **more):
         return pl.pallas_call(
@@ -222,7 +331,7 @@
     payload, ratios, held, slot_weights, ids, mine = call(
         first_kernel,
         (labelled, full, full, per_slot, label, per_slot),
-        (counts, row_block.reshape(1, -1), col_block.reshape(1, -1), blocks, tiles, weight_rows),
+        (counts, *(far(x) for x in (row_block.reshape(1, -1), col_block.reshape(1, -1), blocks, tiles, weight_rows))),
         "first_logs",
         in_specs=[SMEM] + [HBM] * 5,
         scratch_shapes=[
@@ -230,16 +339,45 @@
             lanes,
             lanes,
             pltpu.VMEM(blocks.shape, F32),
+            products,
             dma((4,)),
-            dma((slots // GROUP,)),
+            dma((HALVES,)),
             dma,
         ],
     )
     others = over_tests(payload)
-    parts = over_branches(call(gradient_kernel, labelled, (others, mine, slot_weights, ratios, ids), "gradient"))
-    current, logs, ratios = call(next_kernel, (per_test, per_slot, full), (blocks, held, *parts), "next_logs")
+    made = call(gradient_kernel, labelled, (others, mine, slot_weights, ratios, ids), "gradient")
+    parts = over_branches(made)
+    following_logs = functools.partial(next_kernel, branches)
+    if few_rows:
+        few, sent, places, own = call(
+            plan_kernel,
+            (
+                label,
+                jax.ShapeDtypeStruct((tests * FEW, slots), F32),
+                jax.ShapeDtypeStruct((slots, tests * FEW), F32),
+                jax.ShapeDtypeStruct((slots, slots), F32),
+            ),
+            (others, mine, payload, made),
+            "plan",
+        )
+        current, logs, ratios, rows = call(
+            following_logs,
+            (per_test, per_slot, full, jax.ShapeDtypeStruct((tests, FEW, width), F32)),
+            (blocks, held, *parts, sent),
+            "next_logs",
+            scratch_shapes=[products],
+        )
+        received = lax.all_to_all(rows, "tests", 0, 0)
+        total = call(few_rows_kernel, per_slot, (received, places, own, logs), "few_rows")
+    else:
+        few = jnp.ones(label.shape, F32)
+        current, logs, ratios = call(
+            following_logs, (per_test, per_slot, full), (blocks, held, *parts), "next_logs", scratch_shapes=[products]
+        )
+        total = call(all_rows_kernel, per_slot, (over_tests(logs), others, mine), "all_rows")
     sums, survival = call(
-        last_gradient_kernel, (per_slot, per_slot), (over_tests(logs), others, mine, slot_weights, ratios), "last_gradient"
+        last_gradient_kernel, (labelled, per_slot), (total, slot_weights, ratios, few), "last_gradient"
     )
     last_parts = over_branches(sums)
     tile_grads = call(
@@ -250,10 +388,26 @@
         out_specs=HBM,
         scratch_shapes=[pltpu.VMEM(tiles.shape, F32), dma((slots // GROUP,))],
     )
-    gradient, following = call(
-        functools.partial(last_kernel, branches), (per_test, per_test), (current, *last_parts, *parts), "last_update"
-    )
-    return gradient.reshape(-1), tile_grads, following.reshape(-1)
+    gradient, following, right = call(
+        functools.partial(last_kernel, branches),
+        (per_test, per_test, jax.ShapeDtypeStruct((1,), jnp.int32)),
+        (current, *last_parts, *parts),
+        "last_update",
+        out_specs=(VMEM, VMEM, SMEM),
+    )
+    return right[0], gradient.reshape(-1), tile_grads, following.reshape(-1)
+
+
+def body(tests, branches, *args):
+    if tests != CHUNK:
+        return sweep(tests, branches, False, *args)[1:]
+
+    def again(state):
+        kept, _ = lax.optimization_barrier((args, state[0]))
+        _, *outs = sweep(tests, branches, False, *kept)
+        return jnp.int32(1), *outs
+
+    return lax.while_loop(lambda state: state[0] == 0, again, sweep(tests, branches, True, *args))[1:]
 
 
 def solution(mesh):

time: 54.2 us -> 47.3 us (0.87)
  local copies, waits for them, and re-layouts: 5.59 us -> 0.03 us
  blocking collectives: 30 us -> 27 us
  loops' own time: 0 us -> 0.76 us
    all_to_all x2 -> x1, blocking collectives: 30 us -> 17.4 us  [over_tests(): lax.all_to_all(jnp.broadcast_to(x[None], (tests,) + x.shape), 'tests', 0, 0)]
    all_to_all x0 -> x1, blocking collectives: none -> 9.57 us  [sweep(): received = lax.all_to_all(rows, 'tests', 0, 0)]
    unnamed x10 -> x2, local copies, waits for them, and re-layouts: 5.55 us -> 0.01 us
    another operation x0 -> x1, loops' own time: none -> 0.76 us  [body(): lax.while_loop(lambda state: state[0] == 0, again, sweep(tests, branches,...]
    pallas_call x6 -> x8, Pallas kernels: 10.8 us -> 11.2 us  [call(): pl.pallas_call(kernel, out_shape=outs, in_specs=more.pop('in_specs', [VME...]
  transfers between devices with their start and end apart: 6 -> 6, of which waited for: 2 -> 2; matrix products, arithmetic and copies ran while one was open for 0% -> 0% of each run, Pallas kernels for 5% -> 7%
where the time goes in v3:
time: 47.3 us; the launch traced here: 47.1 us
  blocking collectives  27 us (57%)
  Pallas kernels  11.2 us (24%)
  starting transfers between devices  4.1 us (9%)
  waiting for transfers between devices  2.51 us (5%)
  between operations  1.53 us (3%)
  loops' own time  0.76 us (2%)
    all_to_all x1, blocking collectives, over_tests(): lax.all_to_all(jnp.broadcast_to(x[None], (tests,) + x.shape), 'tests', 0, 0)  17.4 us
    pallas_call x8, Pallas kernels, call(): pl.pallas_call(kernel, out_shape=outs, in_specs=more.pop('in_specs', [VME...  11.2 us
    all_to_all x1, blocking collectives, sweep(): received = lax.all_to_all(rows, 'tests', 0, 0)  9.57 us
    ppermute x6, starting transfers between devices, over_branches(): lax.ppermute(x, 'branches', [(b, b ^ k) for b in range(branches)])  4.1 us
    ppermute x6, waiting for transfers between devices, over_branches(): lax.ppermute(x, 'branches', [(b, b ^ k) for b in range(branches)])  2.51 us
  transfers between devices with their start and end apart: 6, of which 2 were waited for; matrix products, arithmetic and copies ran while one was open for 0% of the time, Pallas kernels for 7%

profile of v3, /device:TPU:0, one launch (start us, length us, event | category | flops | bytes accessed | tf_op | source)
XLA Modules:
  0.0 47.1 jit_solution(10988170138363560791)
XLA Ops:
  1.3 3.0 %first_logs.3 = (f32[72,128]{1,0:T(8,128)S(1)}, f32[64,128,128]{2,1,0:T(8,128)S(1)}, f32[64,128,128]{2,1,0:T(8,128)S(1)}, f32[64,128]{1,0:T(8,128)S(1)}, f32[8,128]{1,0:T(8,128)S(1)}, /*index=5*/f32[64,128]{1,0:T(8,128)S(1)}) custom-call(s32[1]{0:T(128)S(6)} %copy.22.limit, s32[1,64]{1,0:T(1,128)} %bitcast.19, s32[1,64]{1,0:T(1,128)} %bitcast.21, ...), custom_call_target="tpu_custom_call" | custom-call | tf_op jit(solution)/shard_map/first_logs/pallas_call | solution.py:315
  4.3 0.0 copy-start.2
  4.3 17.4 %all_to_all.20.gathered.others = f32[8,72,128]{2,1,0:T(8,128)S(1)} all-to-all(f32[8,72,128]{2,1,0:T(8,128)S(1)} %broadcast_in_dim.6), channel_id=1, replica_groups=mesh['tests'=8,'branches'=4] {'tests'}, dimensions={0} | all-to-all | bytes 589824 | tf_op jit(solution)/shard_map/all_to_all | solution.py:326
  21.7 1.1 %gradient.3.after.refs_0_.refs_4_ = f32[72,128]{1,0:T(8,128)S(1)} custom-call(f32[8,72,128]{2,1,0:T(8,128)S(1)} %all_to_all.20.gathered.others, f32[64,128]{1,0:T(8,128)S(1)} %get-tuple-element.93.mine, f32[64,128]{1,0:T(8,128)S(1)} %get-tuple-element.94.slot_weights, f32[64,128,128]{2,1,0:T(8,128)S(1)} %get-tuple-element.95.ratios, ...), custom_call_target="tpu_custom_call" | custom-call | tf_op jit(solution)/shard_map/gradient/pallas_call | solution.py:315
  22.8 0.0 collective-permute-start.6
  22.9 1.6 %collective-permute-start.7 = (f32[72,128]{1,0:T(8,128)S(1)}, f32[72,128]{1,0:T(8,128)S(1)}, u32[]{:S(2)}, u32[]{:S(2)}) collective-permute-start(f32[72,128]{1,0:T(8,128)S(1)} %gradient.3.after.refs_0_.refs_4_), channel_id=1, source_target_pairs={{0,2},{1,3},{2,0},{3,1},{4,6},{5,7},{6,4},{7,5},{8,10},{9,11},{10,... | collective-permute-start | bytes 110600 | tf_op jit(solution)/shard_map/ppermute | solution.py:329
  24.5 0.3 collective-permute-start.8
  24.8 0.7 %plan.1 = (f32[8,128]{1,0:T(8,128)S(1)}, f32[128,64]{1,0:T(8,128)S(1)}, f32[64,128]{1,0:T(8,128)S(1)}, f32[64,64]{1,0:T(8,128)S(1)}) custom-call(f32[8,72,128]{2,1,0:T(8,128)S(1)} %all_to_all.20.gathered.others, f32[64,128]{1,0:T(8,128)S(1)} %get-tuple-element.93.mine, f32[72,128]{1,0:T(8,128)S(1)} %get-tuple-element.92.payload, ...), custom_call_target="tpu_custom_call" | custom-call | tf_op jit(solution)/shard_map/plan/pallas_call | solution.py:315
  25.4 0.0 collective-permute-done.6.refs_1_.refs_5_
  25.4 1.5 %collective-permute-done.7.refs_2_.refs_6_ = f32[72,128]{1,0:T(8,128)S(1)} collective-permute-done((f32[72,128]{1,0:T(8,128)S(1)}, f32[72,128]{1,0:T(8,128)S(1)}, u32[]{:S(2)}, u32[]{:S(2)}) %collective-permute-start.7) | collective-permute-done | bytes 36896 | tf_op jit(solution)/shard_map/ppermute | solution.py:329
  26.9 1.0 %collective-permute-done.8.refs_3_.refs_7_ = f32[72,128]{1,0:T(8,128)S(1)} collective-permute-done((f32[72,128]{1,0:T(8,128)S(1)}, f32[72,128]{1,0:T(8,128)S(1)}, u32[]{:S(2)}, u32[]{:S(2)}) %collective-permute-start.8) | collective-permute-done | bytes 36896 | tf_op jit(solution)/shard_map/ppermute | solution.py:329
  27.9 0.0 copy-done.2
  27.9 1.8 %next_logs.3 = (f32[128,128]{1,0:T(8,128)S(1)}, f32[64,128]{1,0:T(8,128)S(1)}, f32[64,128,128]{2,1,0:T(8,128)S(1)}, f32[8,16,128]{2,1,0:T(8,128)S(1)}) custom-call(f32[128,128]{1,0:T(8,128)S(1)} %bitcast.16, f32[64,128,128]{2,1,0:T(8,128)S(1)} %get-tuple-element.91.held, f32[72,128]{1,0:T(8,128)S(1)} %gradient.3.after.refs_0_.refs_4_, ...), custom_call_target="tpu_custom_call" | custom-call | tf_op jit(solution)/shard_map/next_logs/pallas_call | solution.py:315
  29.7 9.6 %all_to_all.21.received = f32[8,16,128]{2,1,0:T(8,128)S(1)} all-to-all(f32[8,16,128]{2,1,0:T(8,128)S(1)} %get-tuple-element.99), channel_id=1, replica_groups=mesh['tests'=8,'branches'=4] {'tests'}, dimensions={0} | all-to-all | bytes 131072 | tf_op jit(solution)/shard_map/all_to_all | solution.py:371
  39.3 0.2 few_rows.1.total
  39.5 0.9 %last_gradient.3 = (f32[72,128]{1,0:T(8,128)S(1)}, f32[64,128]{1,0:T(8,128)S(1)}) custom-call(f32[64,128]{1,0:T(8,128)S(1)} %few_rows.1.total, f32[64,128]{1,0:T(8,128)S(1)} %get-tuple-element.94.slot_weights, f32[64,128,128]{2,1,0:T(8,128)S(1)} %get-tuple-element.103.ratios, f32[8,128]{1,0:T(8,128)S(1)} %get-tuple-element.104.few), custom_call_target="tpu_custom_call" | custom-call | tf_op jit(solution)/shard_map/last_gradient/pallas_call | solution.py:315
  40.4 0.9 %collective-permute-start.10 = (f32[72,128]{1,0:T(8,128)S(1)}, f32[72,128]{1,0:T(8,128)S(1)}, u32[]{:S(2)}, u32[]{:S(2)}) collective-permute-start(f32[72,128]{1,0:T(8,128)S(1)} %get-tuple-element.105.refs_0_), channel_id=1, source_target_pairs={{0,2},{1,3},{2,0},{3,1},{4,6},{5,7},{6,4},{7,5},{8,10},{9,11},{10,... | collective-permute-start | bytes 110600 | tf_op jit(solution)/shard_map/ppermute | solution.py:329
  41.3 0.0 collective-permute-start.11
  41.3 1.3 %collective-permute-start.9 = (f32[72,128]{1,0:T(8,128)S(1)}, f32[72,128]{1,0:T(8,128)S(1)}, u32[]{:S(2)}, u32[]{:S(2)}) collective-permute-start(f32[72,128]{1,0:T(8,128)S(1)} %get-tuple-element.105.refs_0_), channel_id=1, source_target_pairs={{0,1},{1,0},{2,3},{3,2},{4,5},{5,4},{6,7},{7,6},{8,9},{9,8},{10,11... | collective-permute-start | bytes 110600 | tf_op jit(solution)/shard_map/ppermute | solution.py:329
  42.6 2.7 %tile_gradients.3 = f32[64,128,128]{2,1,0:T(8,128)} custom-call(f32[128,128]{1,0:T(8,128)S(1)} %get-tuple-element.98.current.blocks, f32[8,128]{1,0:T(8,128)S(1)} %get-tuple-element.96.ids, f32[64,128]{1,0:T(8,128)S(1)} %get-tuple-element.108.survival, f32[64,128,128]{2,1,0:T(8,128)S(1)} %get-tuple-element.91.held), custom_call_target="tpu_custom_call" | custom-call | tf_op jit(solution)/shard_map/tile_gradients/pallas_call | solution.py:315
  45.2 0.0 collective-permute-done.10.refs_2_
  45.2 0.0 collective-permute-done.11.refs_3_
  45.2 0.0 collective-permute-done.9.refs_1_
  45.3 0.9 %last_update.3 = (f32[128,128]{1,0:T(8,128)}, f32[128,128]{1,0:T(8,128)}, s32[1]{0:T(128)}) custom-call(f32[128,128]{1,0:T(8,128)S(1)} %get-tuple-element.98.current.blocks, f32[72,128]{1,0:T(8,128)S(1)} %get-tuple-element.105.refs_0_, f32[72,128]{1,0:T(8,128)S(1)} %collective-permute-done.9.refs_1_, f32[72,128]{1,0:T(8,128)S(1)} %collective-permute-done.10.refs_2_, ...), custom_call_target="tpu_custom_call" | custom-call | tf_op jit(solution)/shard_map/last_update/pallas_call | solution.py:315
  46.2 0.8 %while.13 = (s32[]{:T(128)}, f32[16384]{0:T(1024)}, f32[64,128,128]{2,1,0:T(8,128)}, f32[16384]{0:T(1024)}, f32[16384]{0:T(1024)S(1)}, /*index=5*/f32[64,128,128...) while((s32[]{:T(128)}, f32[16384]{0:T(1024)}, ...), condition=%region_1.0_spmd, body=%region_0.0_spmd | while | flops 1 | bytes 36446640 | solution.py:410
  (1 shorter events, 0.0 us)
Async XLA Ops:
  4.3 23.7 %copy-start.2 = (f32[16384]{0:T(1024)S(1)}, f32[16384]{0:T(1024)}, u32[]{:S(2)}) copy-start(f32[16384]{0:T(1024)} %param.8) | copy-start | bytes 196612
  22.8 2.6 %collective-permute-start.6 = (f32[72,128]{1,0:T(8,128)S(1)}, f32[72,128]{1,0:T(8,128)S(1)}, u32[]{:S(2)}, u32[]{:S(2)}) collective-permute-start(f32[72,128]{1,0:T(8,128)S(1)} %gradient.3.after.refs_0_.refs_4_), channel_id=1, source_target_pairs={{0,1},{1,0},{2,3},{3,2},{4,5},{5,4},{6,7},{7,6},{8,9},{9,8},{10,11... | collective-permute-start | bytes 110600 | tf_op jit(solution)/shard_map/ppermute | solution.py:329
  22.9 4.0 %collective-permute-start.7 = (f32[72,128]{1,0:T(8,128)S(1)}, f32[72,128]{1,0:T(8,128)S(1)}, u32[]{:S(2)}, u32[]{:S(2)}) collective-permute-start(f32[72,128]{1,0:T(8,128)S(1)} %gradient.3.after.refs_0_.refs_4_), channel_id=1, source_target_pairs={{0,2},{1,3},{2,0},{3,1},{4,6},{5,7},{6,4},{7,5},{8,10},{9,11},{10,... | collective-permute-start | bytes 110600 | tf_op jit(solution)/shard_map/ppermute | solution.py:329
  24.5 3.4 %collective-permute-start.8 = (f32[72,128]{1,0:T(8,128)S(1)}, f32[72,128]{1,0:T(8,128)S(1)}, u32[]{:S(2)}, u32[]{:S(2)}) collective-permute-start(f32[72,128]{1,0:T(8,128)S(1)} %gradient.3.after.refs_0_.refs_4_), channel_id=1, source_target_pairs={{0,3},{1,2},{2,1},{3,0},{4,7},{5,6},{6,5},{7,4},{8,11},{9,10},{10,... | collective-permute-start | bytes 110600 | tf_op jit(solution)/shard_map/ppermute | solution.py:329
  40.4 4.9 %collective-permute-start.10 = (f32[72,128]{1,0:T(8,128)S(1)}, f32[72,128]{1,0:T(8,128)S(1)}, u32[]{:S(2)}, u32[]{:S(2)}) collective-permute-start(f32[72,128]{1,0:T(8,128)S(1)} %get-tuple-element.105.refs_0_), channel_id=1, source_target_pairs={{0,2},{1,3},{2,0},{3,1},{4,6},{5,7},{6,4},{7,5},{8,10},{9,11},{10,... | collective-permute-start | bytes 110600 | tf_op jit(solution)/shard_map/ppermute | solution.py:329
  41.3 4.0 %collective-permute-start.11 = (f32[72,128]{1,0:T(8,128)S(1)}, f32[72,128]{1,0:T(8,128)S(1)}, u32[]{:S(2)}, u32[]{:S(2)}) collective-permute-start(f32[72,128]{1,0:T(8,128)S(1)} %get-tuple-element.105.refs_0_), channel_id=1, source_target_pairs={{0,3},{1,2},{2,1},{3,0},{4,7},{5,6},{6,5},{7,4},{8,11},{9,10},{10,... | collective-permute-start | bytes 110600 | tf_op jit(solution)/shard_map/ppermute | solution.py:329
  41.3 4.0 %collective-permute-start.9 = (f32[72,128]{1,0:T(8,128)S(1)}, f32[72,128]{1,0:T(8,128)S(1)}, u32[]{:S(2)}, u32[]{:S(2)}) collective-permute-start(f32[72,128]{1,0:T(8,128)S(1)} %get-tuple-element.105.refs_0_), channel_id=1, source_target_pairs={{0,1},{1,0},{2,3},{3,2},{4,5},{5,4},{6,7},{7,6},{8,9},{9,8},{10,11... | collective-permute-start | bytes 110600 | tf_op jit(solution)/shard_map/ppermute | solution.py:329

commit v4 on v3

--- a/solution.py
+++ b/solution.py
@@ -28,10 +28,11 @@
     return high, middle, low
 
 
-def pick(ones, x):
+def pick(ones, x, count=3):
     width = x.shape[1]
-    parts = jnp.dot(ones, jnp.concatenate(pieces(x), axis=1), preferred_element_type=F32)
-    return parts[:, :width] + (parts[:, width : 2 * width] + parts[:, 2 * width :])
+    parts = jnp.dot(ones, jnp.concatenate(pieces(x)[:count], axis=1), preferred_element_type=F32)
+    low = parts[:, width : 2 * width]
+    return parts[:, :width] + (low if count == 2 else low + parts[:, 2 * width :])
 
 
 def inverse_of(x):
@@ -44,19 +45,14 @@
 
 
 def columns_of(blocks, hits):
-    return [jnp.dot(piece, hits, preferred_element_type=F32) for piece in pieces(blocks.T)]
-
-
-def total_of(columns):
-    high, middle, low = columns
+    high, middle, low = [jnp.dot(piece, hits, preferred_element_type=F32) for piece in pieces(blocks.T)]
     return high + (middle + low)
 
 
 def spread_columns(columns):
-    width, slots = columns[0].shape
-    whole = total_of(columns)
-    stack = jnp.concatenate(columns, axis=1).astype(BF16)
-    shape = (len(columns) * slots, 2 * width)
+    width, slots = columns.shape
+    stack = jnp.concatenate([piece.astype(F32) for piece in pieces(columns)], axis=1).astype(BF16)
+    shape = (stack.shape[1], 2 * width)
     slot = lax.broadcasted_iota(jnp.int32, shape, 0) % slots - lax.broadcasted_iota(jnp.int32, shape, 1) // width
     for s in range(0, slots, 2):
         if (s // 2) % SHARED == SHARED - 1:
@@ -64,8 +60,8 @@
             yield both[:, :width]
             yield both[:, width:]
         else:
-            yield whole[:, s : s + 1]
-            yield whole[:, s + 1 : s + 2]
+            yield columns[:, s : s + 1]
+            yield columns[:, s + 1 : s + 2]
 
 
 def slots_pass(columns, tiles, ratios, products, before=lambda s: None):
@@ -89,7 +85,7 @@
     return total
 
 
-def first_kernel(limit, rows, cols, blocks, tiles, weights, payload, ratios, held, slot_weights, ids, mine, near, row_lanes, col_lanes, own, products, sems, tile_sem, weight_sem):
+def first_kernel(limit, rows, cols, blocks, tiles, weights, payload, ratios, held, slot_weights, ids, mine, down, picked, near, row_lanes, col_lanes, own, products, sems, tile_sem, weight_sem):
     slots, width = held.shape[0], held.shape[1]
     small = [
         pltpu.make_async_copy(source, target, sems.at[i])
@@ -114,7 +110,9 @@
     mine[...] = jnp.broadcast_to(jnp.where(live, col_lanes[...], -2).astype(F32), (width, slots)).T
     own_ids = row_lanes[...].astype(F32)
     ids[...] = jnp.broadcast_to(jnp.concatenate([own_ids] * (width // slots), axis=1), (EXTRA, width))
+    down[...] = jnp.broadcast_to(own_ids, (width, slots)).T
     columns = columns_of(own[...], hits_of(own_ids, own.shape[0]))
+    picked[...] = columns.T
 
     def arrive(s):
         if s % chunk == 0:
@@ -244,49 +242,74 @@
     return current + (select_cap - current) * rate / (1.0 + rate)
 
 
-def gradient_of(parts, ids, test_rows):
-    slots = ids[0].shape[0] - EXTRA
-    sums = [pick(hits_of(i[slots : slots + 1, :slots], test_rows), p[:slots, :]) for p, i in zip(parts, ids)]
-    while len(sums) > 1:
-        sums = [a + b for a, b in zip(sums[::2], sums[1::2])]
-    return sums[0]
-
-
-def next_kernel(branches, blocks, held, *refs):
-    parts, refs = refs[:branches], refs[branches:]
-    *sent, current, logs, ratios, out, products = refs if len(refs) == 6 else (*refs[:3], None, refs[3])
-    test_rows, slots = blocks.shape[0], held.shape[0]
-    current[...] = advance(blocks[...], gradient_of(parts, parts, test_rows))
-    columns = columns_of(current[...], hits_of(parts[0][slots : slots + 1, :slots], test_rows))
-    slots_pass(columns, held, ratios, products)
+def in_turn(refs):
+    me = lax.axis_index("branches")
+    return [(me ^ k, ref) for k, ref in enumerate(refs)]
+
+
+def lanes_of(rows, slots):
+    width = rows[0].shape[1]
+    each = width // slots
+    lane = lax.broadcasted_iota(jnp.int32, (1, width), 1)
+    joined = []
+    for start in range(0, len(rows), each):
+        row = rows[start]
+        for k in range(1, each):
+            row = jnp.where(lane < k * slots, row, rows[start + k])
+        joined.append(row)
+    return jnp.concatenate(joined, axis=1)
+
+
+def next_kernel(branches, held, down, picked, *refs):
+    parts, refs = refs[:branches][::-1], refs[branches:]
+    *sent, columns, logs, ratios, out, products = refs if len(refs) == 6 else (*refs[:3], None, refs[3])
+    slots = held.shape[0]
+    ids = lanes_of([p[slots : slots + 1, :] for p in parts], slots)
+    same = jnp.concatenate([down[...]] * (ids.shape[1] // down.shape[1]), axis=1) == ids
+    gradient = pick(jnp.where(same, 1.0, 0.0).astype(BF16), jnp.concatenate([p[:slots, :] for p in parts], axis=0), 2)
+    now = advance(picked[...], gradient).T
+    columns[...] = now
+    slots_pass(now, held, ratios, products)
     rows = logs_of(products)
     logs[...] = rows
     if sent:
         out[...] = pick(sent[0][...].astype(BF16), rows).reshape(out.shape)
 
 
-def tile_kernel(blocks, ids, survival, held, out, made, sems):
-    slots = held.shape[0]
-    columns = total_of(columns_of(blocks[...], hits_of(ids[:1, :slots], blocks.shape[0])))
+def tile_kernel(blocks, columns, survival, held, *refs):
+    *parts, out, current, hits, made, table, rows, sems = refs
+    slots, width = survival.shape
+    for place, part in in_turn(parts):
+        table[pl.ds(place, 1), :] = part[slots : slots + 1, :]
+        rows[place] = part[:slots, :]
+    now = columns[...]
     copies = []
     for s in range(slots):
-        share = columns[:, s : s + 1]
+        share = now[:, s : s + 1]
         made[s] = survival[s : s + 1, :] * share * inverse_of(1.0 - share * held[s])
         if s % GROUP == GROUP - 1:
-            part = pl.ds(s + 1 - GROUP, GROUP)
-            copies.append(pltpu.make_async_copy(made.at[part], out.at[part], sems.at[s // GROUP]))
+            group = pl.ds(s + 1 - GROUP, GROUP)
+            copies.append(pltpu.make_async_copy(made.at[group], out.at[group], sems.at[s // GROUP]))
             copies[-1].start()
+    ids = lanes_of([table[k : k + 1, :] for k in range(len(parts))], slots)
+    every = hits_of(ids, blocks.shape[0])
+    hits[...] = every.astype(F32)
+    gradient = pick(every, rows[...].reshape(-1, width), 2)
+    current[...] = advance(blocks[...], gradient)
     for copy in copies:
         copy.wait()
 
 
-def last_kernel(branches, current, *refs):
-    *given, gradient, following, few = refs
-    parts, ids = given[:branches], given[branches:]
-    total = gradient_of(parts, ids, current.shape[0])
+def last_kernel(current, hits, *refs):
+    *given, gradient, following, few, rows = refs
+    first, second, *others = given
+    parts = [first, second, *others[::-1]]
+    slots = rows.shape[1]
+    for place, part in in_turn(parts):
+        rows[place] = part[:slots, :]
+    total = pick(hits[...].astype(BF16), rows[...].reshape(-1, rows.shape[2]), 2)
     gradient[...] = total
     following[...] = advance(current[...], total)
-    slots = parts[0].shape[0] - EXTRA
     fewest = functools.reduce(jnp.minimum, [p[slots : slots + 1, :] for p in parts])
     few[0] = jnp.min(fewest).astype(jnp.int32)
 
@@ -306,6 +329,7 @@
     labelled = jax.ShapeDtypeStruct((slots + EXTRA, width), F32)
     label = jax.ShapeDtypeStruct((EXTRA, width), F32)
     per_test = jax.ShapeDtypeStruct(blocks.shape, F32)
+    per_column = jax.ShapeDtypeStruct((width, slots), F32)
     lanes = pltpu.VMEM((1, slots), jnp.int32)
     products = pltpu.VMEM((8 * slots, width), F32)
     dma = pltpu.SemaphoreType.DMA
@@ -328,9 +352,9 @@
     def over_branches(x):
         return [x] + [lax.ppermute(x, "branches", [(b, b ^ k) for b in range(branches)]) for k in range(1, branches)]
 
-    payload, ratios, held, slot_weights, ids, mine = call(
+    payload, ratios, held, slot_weights, ids, mine, down, picked = call(
         first_kernel,
-        (labelled, full, full, per_slot, label, per_slot),
+        (labelled, full, full, per_slot, label, per_slot, per_slot, per_slot),
         (counts, *(far(x) for x in (row_block.reshape(1, -1), col_block.reshape(1, -1), blocks, tiles, weight_rows))),
         "first_logs",
         in_specs=[SMEM] + [HBM] * 5,
@@ -361,10 +385,10 @@
             (others, mine, payload, made),
             "plan",
         )
-        current, logs, ratios, rows = call(
+        columns, logs, ratios, rows = call(
             following_logs,
-            (per_test, per_slot, full, jax.ShapeDtypeStruct((tests, FEW, width), F32)),
-            (blocks, held, *parts, sent),
+            (per_column, per_slot, full, jax.ShapeDtypeStruct((tests, FEW, width), F32)),
+            (held, down, picked, *parts[::-1], sent),
             "next_logs",
             scratch_shapes=[products],
         )
@@ -372,28 +396,39 @@
         total = call(few_rows_kernel, per_slot, (received, places, own, logs), "few_rows")
     else:
         few = jnp.ones(label.shape, F32)
-        current, logs, ratios = call(
-            following_logs, (per_test, per_slot, full), (blocks, held, *parts), "next_logs", scratch_shapes=[products]
+        columns, logs, ratios = call(
+            following_logs,
+            (per_column, per_slot, full),
+            (held, down, picked, *parts[::-1]),
+            "next_logs",
+            scratch_shapes=[products],
         )
         total = call(all_rows_kernel, per_slot, (over_tests(logs), others, mine), "all_rows")
     sums, survival = call(
         last_gradient_kernel, (labelled, per_slot), (total, slot_weights, ratios, few), "last_gradient"
     )
     last_parts = over_branches(sums)
-    tile_grads = call(
+    part_rows = pltpu.VMEM((branches, slots, width), F32)
+    tile_grads, current, hits = call(
         tile_kernel,
-        full,
-        (current, ids, survival, held),
+        (full, per_test, jax.ShapeDtypeStruct((blocks.shape[0], branches * slots), F32)),
+        (blocks, columns, survival, held, *parts),
         "tile_gradients",
-        out_specs=HBM,
-        scratch_shapes=[pltpu.VMEM(tiles.shape, F32), dma((slots // GROUP,))],
+        out_specs=(HBM, VMEM, VMEM),
+        scratch_shapes=[
+            pltpu.VMEM(tiles.shape, F32),
+            pltpu.VMEM((8, width), F32),
+            part_rows,
+            dma((slots // GROUP,)),
+        ],
     )
     gradient, following, right = call(
-        functools.partial(last_kernel, branches),
+        last_kernel,
         (per_test, per_test, jax.ShapeDtypeStruct((1,), jnp.int32)),
-        (current, *last_parts, *parts),
+        (current, hits, *last_parts[:2], *last_parts[:1:-1]),
         "last_update",
         out_specs=(VMEM, VMEM, SMEM),
+        scratch_shapes=[part_rows],
     )
     return right[0], gradient.reshape(-1), tile_grads, following.reshape(-1)
 

time: 47.3 us -> 46.7 us (0.987)
  blocking collectives: 27 us -> 27.8 us
  waiting for transfers between devices: 2.51 us -> 1.87 us
  Pallas kernels: 11.2 us -> 10.6 us
    all_to_all x1, blocking collectives: 9.57 us -> 10.4 us  [sweep(): received = lax.all_to_all(rows, 'tests', 0, 0)]
    ppermute x6, waiting for transfers between devices: 2.51 us -> 1.87 us  [over_branches(): lax.ppermute(x, 'branches', [(b, b ^ k) for b in range(branches)])]
    pallas_call x8, Pallas kernels: 11.2 us -> 10.6 us  [call(): pl.pallas_call(kernel, out_shape=outs, in_specs=more.pop('in_specs', [VME...]
  transfers between devices with their start and end apart: 6 -> 6, of which waited for: 2 -> 3; matrix products, arithmetic and copies ran while one was open for 0% -> 0% of each run, Pallas kernels for 7% -> 6%
where the time goes in v4:
time: 46.7 us; the launch traced here: 46.5 us
  blocking collectives  27.8 us (60%)
  Pallas kernels  10.6 us (23%)
  starting transfers between devices  3.8 us (8%)
  waiting for transfers between devices  1.87 us (4%)
  between operations  1.52 us (3%)
  loops' own time  0.87 us (2%)
    all_to_all x1, blocking collectives, over_tests(): lax.all_to_all(jnp.broadcast_to(x[None], (tests,) + x.shape), 'tests', 0, 0)  17.4 us
    pallas_call x8, Pallas kernels, call(): pl.pallas_call(kernel, out_shape=outs, in_specs=more.pop('in_specs', [VME...  10.6 us
    all_to_all x1, blocking collectives, sweep(): received = lax.all_to_all(rows, 'tests', 0, 0)  10.4 us
    ppermute x6, starting transfers between devices, over_branches(): lax.ppermute(x, 'branches', [(b, b ^ k) for b in range(branches)])  3.8 us
    ppermute x6, waiting for transfers between devices, over_branches(): lax.ppermute(x, 'branches', [(b, b ^ k) for b in range(branches)])  1.87 us
  transfers between devices with their start and end apart: 6, of which 3 were waited for; matrix products, arithmetic and copies ran while one was open for 0% of the time, Pallas kernels for 6%

profile of v4, /device:TPU:0, one launch (start us, length us, event | category | flops | bytes accessed | tf_op | source)
XLA Modules:
  0.0 46.5 jit_solution(2361157982711857900)
XLA Ops:
  1.3 3.1 %first_logs.3 = (f32[72,128]{1,0:T(8,128)S(1)}, f32[64,128,128]{2,1,0:T(8,128)S(1)}, f32[64,128,128]{2,1,0:T(8,128)S(1)}, f32[64,128]{1,0:T(8,128)S(1)}, f32[8,1...) custom-call(s32[1]{0:T(128)S(6)} %copy.22.limit, s32[1,64]{1,0:T(1,128)} %bitcast.19, ...), custom_call_target="tpu_custom_call" | custom-call | tf_op jit(solution)/shard_map/first_logs/pallas_call | solution.py:339
  4.4 17.4 %all_to_all.20.gathered.others = f32[8,72,128]{2,1,0:T(8,128)S(1)} all-to-all(f32[8,72,128]{2,1,0:T(8,128)S(1)} %broadcast_in_dim.6), channel_id=1, replica_groups=mesh['tests'=8,'branches'=4] {'tests'}, dimensions={0} | all-to-all | bytes 589824 | tf_op jit(solution)/shard_map/all_to_all | solution.py:350
  21.8 1.1 %gradient.3.after.refs_3_.refs_0_ = f32[72,128]{1,0:T(8,128)S(1)} custom-call(f32[8,72,128]{2,1,0:T(8,128)S(1)} %all_to_all.20.gathered.others, f32[64,128]{1,0:T(8,128)S(1)} %get-tuple-element.105.mine, f32[64,128]{1,0:T(8,128)S(1)} %get-tuple-element.106.slot_weights, f32[64,128,128]{2,1,0:T(8,128)S(1)} %get-tuple-element.107.ratios, ...), custom_call_target="tpu_custom_call" | custom-call | tf_op jit(solution)/shard_map/gradient/pallas_call | solution.py:339
  22.9 0.0 collective-permute-start.6
  23.0 1.6 %collective-permute-start.7 = (f32[72,128]{1,0:T(8,128)S(1)}, f32[72,128]{1,0:T(8,128)S(1)}, u32[]{:S(2)}, u32[]{:S(2)}) collective-permute-start(f32[72,128]{1,0:T(8,128)S(1)} %gradient.3.after.refs_3_.refs_0_), channel_id=1, source_target_pairs={{0,2},{1,3},{2,0},{3,1},{4,6},{5,7},{6,4},{7,5},{8,10},{9,11},{10,... | collective-permute-start | bytes 110600 | tf_op jit(solution)/shard_map/ppermute | solution.py:353
  24.5 0.3 collective-permute-start.8
  24.8 0.7 %plan.1 = (f32[8,128]{1,0:T(8,128)S(1)}, f32[128,64]{1,0:T(8,128)S(1)}, f32[64,128]{1,0:T(8,128)S(1)}, f32[64,64]{1,0:T(8,128)S(1)}) custom-call(f32[8,72,128]{2,1,0:T(8,128)S(1)} %all_to_all.20.gathered.others, f32[64,128]{1,0:T(8,128)S(1)} %get-tuple-element.105.mine, f32[72,128]{1,0:T(8,128)S(1)} %get-tuple-element.104.payload, ...), custom_call_target="tpu_custom_call" | custom-call | tf_op jit(solution)/shard_map/plan/pallas_call | solution.py:339
  25.5 1.2 %collective-permute-done.6.refs_0_.refs_3_ = f32[72,128]{1,0:T(8,128)S(1)} collective-permute-done((f32[72,128]{1,0:T(8,128)S(1)}, f32[72,128]{1,0:T(8,128)S(1)}, u32[]{:S(2)}, u32[]{:S(2)}) %collective-permute-start.6) | collective-permute-done | bytes 36896 | tf_op jit(solution)/shard_map/ppermute | solution.py:353
  26.6 0.5 %collective-permute-done.7.refs_1_.refs_2_ = f32[72,128]{1,0:T(8,128)S(1)} collective-permute-done((f32[72,128]{1,0:T(8,128)S(1)}, f32[72,128]{1,0:T(8,128)S(1)}, u32[]{:S(2)}, u32[]{:S(2)}) %collective-permute-start.7) | collective-permute-done | bytes 36896 | tf_op jit(solution)/shard_map/ppermute | solution.py:353
  27.1 0.0 collective-permute-done.8.refs_2_.refs_1_
  27.1 0.0 copy-start.2
  27.1 1.6 %next_logs.3 = (f32[128,64]{1,0:T(8,128)S(1)}, f32[64,128]{1,0:T(8,128)S(1)}, f32[64,128,128]{2,1,0:T(8,128)S(1)}, f32[8,16,128]{2,1,0:T(8,128)S(1)}) custom-call(f32[64,128,128]{2,1,0:T(8,128)S(1)} %get-tuple-element.101.held, f32[64,128]{1,0:T(8,128)S(1)} %get-tuple-element.102.down, f32[64,128]{1,0:T(8,128)S(1)} %get-tuple-element.103.picked, ...), custom_call_target="tpu_custom_call" | custom-call | tf_op jit(solution)/shard_map/next_logs/pallas_call | solution.py:339
  28.7 10.4 %all_to_all.21.received = f32[8,16,128]{2,1,0:T(8,128)S(1)} all-to-all(f32[8,16,128]{2,1,0:T(8,128)S(1)} %get-tuple-element.111), channel_id=1, replica_groups=mesh['tests'=8,'branches'=4] {'tests'}, dimensions={0} | all-to-all | bytes 131072 | tf_op jit(solution)/shard_map/all_to_all | solution.py:395
  39.1 0.2 few_rows.1.total
  39.3 0.9 %last_gradient.3 = (f32[72,128]{1,0:T(8,128)S(1)}, f32[64,128]{1,0:T(8,128)S(1)}) custom-call(f32[64,128]{1,0:T(8,128)S(1)} %few_rows.1.total, f32[64,128]{1,0:T(8,128)S(1)} %get-tuple-element.106.slot_weights, f32[64,128,128]{2,1,0:T(8,128)S(1)} %get-tuple-element.115.ratios, f32[8,128]{1,0:T(8,128)S(1)} %get-tuple-element.116.few), custom_call_target="tpu_custom_call" | custom-call | tf_op jit(solution)/shard_map/last_gradient/pallas_call | solution.py:339
  40.2 0.1 collective-permute-start.10
  40.2 1.0 %collective-permute-start.11 = (f32[72,128]{1,0:T(8,128)S(1)}, f32[72,128]{1,0:T(8,128)S(1)}, u32[]{:S(2)}, u32[]{:S(2)}) collective-permute-start(f32[72,128]{1,0:T(8,128)S(1)} %get-tuple-element.120.refs_0_), channel_id=1, source_target_pairs={{0,2},{1,3},{2,0},{3,1},{4,6},{5,7},{6,4},{7,5},{8,10},{9,11},{10,... | collective-permute-start | bytes 110600 | tf_op jit(solution)/shard_map/ppermute | solution.py:353
  41.2 0.9 %collective-permute-start.9 = (f32[72,128]{1,0:T(8,128)S(1)}, f32[72,128]{1,0:T(8,128)S(1)}, u32[]{:S(2)}, u32[]{:S(2)}) collective-permute-start(f32[72,128]{1,0:T(8,128)S(1)} %get-tuple-element.120.refs_0_), channel_id=1, source_target_pairs={{0,1},{1,0},{2,3},{3,2},{4,5},{5,4},{6,7},{7,6},{8,9},{9,8},{10,11... | collective-permute-start | bytes 110600 | tf_op jit(solution)/shard_map/ppermute | solution.py:353
  42.1 0.0 copy-done.2
  42.1 2.3 %tile_gradients.3 = (f32[64,128,128]{2,1,0:T(8,128)}, f32[128,128]{1,0:T(8,128)S(1)}, f32[128,256]{1,0:T(8,128)S(1)}) custom-call(f32[128,128]{1,0:T(8,128)S(1)} %bitcast.16, f32[128,64]{1,0:T(8,128)S(1)} %get-tuple-element.110.columns, f32[64,128]{1,0:T(8,128)S(1)} %get-tuple-element.117.survival, f32[64,128,128]{2,1,0:T(8,128)S(1)} %get-tuple-element.101.held, ...), custom_call_target="tpu_custom_call" | custom-call | tf_op jit(solution)/shard_map/tile_gradients/pallas_call | solution.py:339
  44.4 0.0 collective-permute-done.10.refs_2_
  44.4 0.2 collective-permute-done.11.refs_3_
  44.6 0.0 collective-permute-done.9.refs_1_
  44.6 0.9 %last_update.3 = (f32[128,128]{1,0:T(8,128)}, f32[128,128]{1,0:T(8,128)}, s32[1]{0:T(128)}) custom-call(f32[128,128]{1,0:T(8,128)S(1)} %get-tuple-element.118.current, f32[128,256]{1,0:T(8,128)S(1)} %get-tuple-element.119.hits, f32[72,128]{1,0:T(8,128)S(1)} %get-tuple-element.120.refs_0_, f32[72,128]{1,0:T(8,128)S(1)} %collective-permute-done.9.refs_1_, ...), custom_call_target="tpu_custom_call" | custom-call | tf_op jit(solution)/shard_map/last_update/pallas_call | solution.py:339
  45.5 0.9 %while.13 = (s32[]{:T(128)}, f32[16384]{0:T(1024)}, f32[64,128,128]{2,1,0:T(8,128)}, f32[16384]{0:T(1024)}, f32[16384]{0:T(1024)S(1)}, /*index=5*/f32[64,128,128...) while((s32[]{:T(128)}, f32[16384]{0:T(1024)}, ...), condition=%region_1.0_spmd, body=%region_0.0_spmd | while | flops 1 | bytes 36446640 | solution.py:445
  (1 shorter events, 0.0 us)
Async XLA Ops:
  22.9 3.7 %collective-permute-start.6 = (f32[72,128]{1,0:T(8,128)S(1)}, f32[72,128]{1,0:T(8,128)S(1)}, u32[]{:S(2)}, u32[]{:S(2)}) collective-permute-start(f32[72,128]{1,0:T(8,128)S(1)} %gradient.3.after.refs_3_.refs_0_), channel_id=1, source_target_pairs={{0,3},{1,2},{2,1},{3,0},{4,7},{5,6},{6,5},{7,4},{8,11},{9,10},{10,... | collective-permute-start | bytes 110600 | tf_op jit(solution)/shard_map/ppermute | solution.py:353
  23.0 4.2 %collective-permute-start.7 = (f32[72,128]{1,0:T(8,128)S(1)}, f32[72,128]{1,0:T(8,128)S(1)}, u32[]{:S(2)}, u32[]{:S(2)}) collective-permute-start(f32[72,128]{1,0:T(8,128)S(1)} %gradient.3.after.refs_3_.refs_0_), channel_id=1, source_target_pairs={{0,2},{1,3},{2,0},{3,1},{4,6},{5,7},{6,4},{7,5},{8,10},{9,11},{10,... | collective-permute-start | bytes 110600 | tf_op jit(solution)/shard_map/ppermute | solution.py:353
  24.5 2.6 %collective-permute-start.8 = (f32[72,128]{1,0:T(8,128)S(1)}, f32[72,128]{1,0:T(8,128)S(1)}, u32[]{:S(2)}, u32[]{:S(2)}) collective-permute-start(f32[72,128]{1,0:T(8,128)S(1)} %gradient.3.after.refs_3_.refs_0_), channel_id=1, source_target_pairs={{0,1},{1,0},{2,3},{3,2},{4,5},{5,4},{6,7},{7,6},{8,9},{9,8},{10,11... | collective-permute-start | bytes 110600 | tf_op jit(solution)/shard_map/ppermute | solution.py:353
  27.1 15.0 %copy-start.2 = (f32[16384]{0:T(1024)S(1)}, f32[16384]{0:T(1024)}, u32[]{:S(2)}) copy-start(f32[16384]{0:T(1024)} %param.8) | copy-start | bytes 196612
  40.2 4.2 %collective-permute-start.10 = (f32[72,128]{1,0:T(8,128)S(1)}, f32[72,128]{1,0:T(8,128)S(1)}, u32[]{:S(2)}, u32[]{:S(2)}) collective-permute-start(f32[72,128]{1,0:T(8,128)S(1)} %get-tuple-element.120.refs_0_), channel_id=1, source_target_pairs={{0,3},{1,2},{2,1},{3,0},{4,7},{5,6},{6,5},{7,4},{8,11},{9,10},{10,... | collective-permute-start | bytes 110600 | tf_op jit(solution)/shard_map/ppermute | solution.py:353
  40.2 4.4 %collective-permute-start.11 = (f32[72,128]{1,0:T(8,128)S(1)}, f32[72,128]{1,0:T(8,128)S(1)}, u32[]{:S(2)}, u32[]{:S(2)}) collective-permute-start(f32[72,128]{1,0:T(8,128)S(1)} %get-tuple-element.120.refs_0_), channel_id=1, source_target_pairs={{0,2},{1,3},{2,0},{3,1},{4,6},{5,7},{6,4},{7,5},{8,10},{9,11},{10,... | collective-permute-start | bytes 110600 | tf_op jit(solution)/shard_map/ppermute | solution.py:353
  41.2 3.4 %collective-permute-start.9 = (f32[72,128]{1,0:T(8,128)S(1)}, f32[72,128]{1,0:T(8,128)S(1)}, u32[]{:S(2)}, u32[]{:S(2)}) collective-permute-start(f32[72,128]{1,0:T(8,128)S(1)} %get-tuple-element.120.refs_0_), channel_id=1, source_target_pairs={{0,1},{1,0},{2,3},{3,2},{4,5},{5,4},{6,7},{7,6},{8,9},{9,8},{10,11... | collective-permute-start | bytes 110600 | tf_op jit(solution)/shard_map/ppermute | solution.py:353

commit v5 on v4

--- a/solution.py
+++ b/solution.py
@@ -424,7 +424,7 @@
     )
     gradient, following, right = call(
         last_kernel,
-        (per_test, per_test, jax.ShapeDtypeStruct((1,), jnp.int32)),
+        (per_test, per_test, pltpu.SMEM((1,), jnp.int32)),
         (current, hits, *last_parts[:2], *last_parts[:1:-1]),
         "last_update",
         out_specs=(VMEM, VMEM, SMEM),
@@ -440,9 +440,10 @@
     def again(state):
         kept, _ = lax.optimization_barrier((args, state[0]))
         _, *outs = sweep(tests, branches, False, *kept)
-        return jnp.int32(1), *outs
-
-    return lax.while_loop(lambda state: state[0] == 0, again, sweep(tests, branches, True, *args))[1:]
+        return state[0] != state[0], *outs
+
+    right, *outs = sweep(tests, branches, True, *args)
+    return lax.while_loop(lambda state: state[0], again, (right == 0, *outs))[1:]
 
 
 def solution(mesh):

time: 46.7 us -> 45.6 us (0.976)
  loops' own time: 0.87 us -> 0.01 us
    another operation x1, loops' own time: 0.87 us -> 0.01 us  [body(): lax.while_loop(lambda state: state[0], again, (right == 0, *outs))[1:]]
where the time goes in v5:
time: 45.6 us; the launch traced here: 45.4 us
  blocking collectives  27.8 us (61%)
  Pallas kernels  10.6 us (23%)
  starting transfers between devices  3.8 us (8%)
  waiting for transfers between devices  1.87 us (4%)
  between operations  1.35 us (3%)
    all_to_all x1, blocking collectives, over_tests(): lax.all_to_all(jnp.broadcast_to(x[None], (tests,) + x.shape), 'tests', 0, 0)  17.4 us
    pallas_call x8, Pallas kernels, call(): pl.pallas_call(kernel, out_shape=outs, in_specs=more.pop('in_specs', [VME...  10.6 us
    all_to_all x1, blocking collectives, sweep(): received = lax.all_to_all(rows, 'tests', 0, 0)  10.4 us
    ppermute x6, starting transfers between devices, over_branches(): lax.ppermute(x, 'branches', [(b, b ^ k) for b in range(branches)])  3.8 us
    ppermute x6, waiting for transfers between devices, over_branches(): lax.ppermute(x, 'branches', [(b, b ^ k) for b in range(branches)])  1.87 us
  transfers between devices with their start and end apart: 6, of which 3 were waited for; matrix products, arithmetic and copies ran while one was open for 0% of the time, Pallas kernels for 6%

profile of v5, /device:TPU:0, one launch (start us, length us, event | category | flops | bytes accessed | tf_op | source)
XLA Modules:
  0.0 45.4 jit_solution(17477131431121542455)
XLA Ops:
  1.3 3.1 %first_logs.3 = (f32[72,128]{1,0:T(8,128)S(1)}, f32[64,128,128]{2,1,0:T(8,128)S(1)}, f32[64,128,128]{2,1,0:T(8,128)S(1)}, f32[64,128]{1,0:T(8,128)S(1)}, f32[8,1...) custom-call(s32[1]{0:T(128)S(6)} %copy.22.limit, s32[1,64]{1,0:T(1,128)} %bitcast.19, ...), custom_call_target="tpu_custom_call" | custom-call | tf_op jit(solution)/shard_map/first_logs/pallas_call | solution.py:339
  4.4 17.4 %all_to_all.20.gathered.others = f32[8,72,128]{2,1,0:T(8,128)S(1)} all-to-all(f32[8,72,128]{2,1,0:T(8,128)S(1)} %broadcast_in_dim.6), channel_id=1, replica_groups=mesh['tests'=8,'branches'=4] {'tests'}, dimensions={0} | all-to-all | bytes 589824 | tf_op jit(solution)/shard_map/all_to_all | solution.py:350
  21.8 1.1 %gradient.3.after.refs_3_.refs_0_ = f32[72,128]{1,0:T(8,128)S(1)} custom-call(f32[8,72,128]{2,1,0:T(8,128)S(1)} %all_to_all.20.gathered.others, f32[64,128]{1,0:T(8,128)S(1)} %get-tuple-element.105.mine, f32[64,128]{1,0:T(8,128)S(1)} %get-tuple-element.106.slot_weights, f32[64,128,128]{2,1,0:T(8,128)S(1)} %get-tuple-element.107.ratios, ...), custom_call_target="tpu_custom_call" | custom-call | tf_op jit(solution)/shard_map/gradient/pallas_call | solution.py:339
  22.9 0.0 collective-permute-start.6
  22.9 1.6 %collective-permute-start.7 = (f32[72,128]{1,0:T(8,128)S(1)}, f32[72,128]{1,0:T(8,128)S(1)}, u32[]{:S(2)}, u32[]{:S(2)}) collective-permute-start(f32[72,128]{1,0:T(8,128)S(1)} %gradient.3.after.refs_3_.refs_0_), channel_id=1, source_target_pairs={{0,2},{1,3},{2,0},{3,1},{4,6},{5,7},{6,4},{7,5},{8,10},{9,11},{10,... | collective-permute-start | bytes 110600 | tf_op jit(solution)/shard_map/ppermute | solution.py:353
  24.5 0.3 collective-permute-start.8
  24.8 0.7 %plan.1 = (f32[8,128]{1,0:T(8,128)S(1)}, f32[128,64]{1,0:T(8,128)S(1)}, f32[64,128]{1,0:T(8,128)S(1)}, f32[64,64]{1,0:T(8,128)S(1)}) custom-call(f32[8,72,128]{2,1,0:T(8,128)S(1)} %all_to_all.20.gathered.others, f32[64,128]{1,0:T(8,128)S(1)} %get-tuple-element.105.mine, f32[72,128]{1,0:T(8,128)S(1)} %get-tuple-element.104.payload, ...), custom_call_target="tpu_custom_call" | custom-call | tf_op jit(solution)/shard_map/plan/pallas_call | solution.py:339
  25.4 1.2 %collective-permute-done.6.refs_0_.refs_3_ = f32[72,128]{1,0:T(8,128)S(1)} collective-permute-done((f32[72,128]{1,0:T(8,128)S(1)}, f32[72,128]{1,0:T(8,128)S(1)}, u32[]{:S(2)}, u32[]{:S(2)}) %collective-permute-start.6) | collective-permute-done | bytes 36896 | tf_op jit(solution)/shard_map/ppermute | solution.py:353
  26.6 0.5 %collective-permute-done.7.refs_1_.refs_2_ = f32[72,128]{1,0:T(8,128)S(1)} collective-permute-done((f32[72,128]{1,0:T(8,128)S(1)}, f32[72,128]{1,0:T(8,128)S(1)}, u32[]{:S(2)}, u32[]{:S(2)}) %collective-permute-start.7) | collective-permute-done | bytes 36896 | tf_op jit(solution)/shard_map/ppermute | solution.py:353
  27.1 0.0 collective-permute-done.8.refs_2_.refs_1_
  27.1 0.0 copy-start.2
  27.1 1.6 %next_logs.3 = (f32[128,64]{1,0:T(8,128)S(1)}, f32[64,128]{1,0:T(8,128)S(1)}, f32[64,128,128]{2,1,0:T(8,128)S(1)}, f32[8,16,128]{2,1,0:T(8,128)S(1)}) custom-call(f32[64,128,128]{2,1,0:T(8,128)S(1)} %get-tuple-element.101.held, f32[64,128]{1,0:T(8,128)S(1)} %get-tuple-element.102.down, f32[64,128]{1,0:T(8,128)S(1)} %get-tuple-element.103.picked, ...), custom_call_target="tpu_custom_call" | custom-call | tf_op jit(solution)/shard_map/next_logs/pallas_call | solution.py:339
  28.7 10.4 %all_to_all.21.received = f32[8,16,128]{2,1,0:T(8,128)S(1)} all-to-all(f32[8,16,128]{2,1,0:T(8,128)S(1)} %get-tuple-element.111), channel_id=1, replica_groups=mesh['tests'=8,'branches'=4] {'tests'}, dimensions={0} | all-to-all | bytes 131072 | tf_op jit(solution)/shard_map/all_to_all | solution.py:395
  39.1 0.2 few_rows.1.total
  39.3 0.9 %last_gradient.3 = (f32[72,128]{1,0:T(8,128)S(1)}, f32[64,128]{1,0:T(8,128)S(1)}) custom-call(f32[64,128]{1,0:T(8,128)S(1)} %few_rows.1.total, f32[64,128]{1,0:T(8,128)S(1)} %get-tuple-element.106.slot_weights, f32[64,128,128]{2,1,0:T(8,128)S(1)} %get-tuple-element.115.ratios, f32[8,128]{1,0:T(8,128)S(1)} %get-tuple-element.116.few), custom_call_target="tpu_custom_call" | custom-call | tf_op jit(solution)/shard_map/last_gradient/pallas_call | solution.py:339
  40.1 0.1 collective-permute-start.10
  40.2 0.9 %collective-permute-start.11 = (f32[72,128]{1,0:T(8,128)S(1)}, f32[72,128]{1,0:T(8,128)S(1)}, u32[]{:S(2)}, u32[]{:S(2)}) collective-permute-start(f32[72,128]{1,0:T(8,128)S(1)} %get-tuple-element.120.refs_0_), channel_id=1, source_target_pairs={{0,2},{1,3},{2,0},{3,1},{4,6},{5,7},{6,4},{7,5},{8,10},{9,11},{10,... | collective-permute-start | bytes 110600 | tf_op jit(solution)/shard_map/ppermute | solution.py:353
  41.1 0.9 %collective-permute-start.9 = (f32[72,128]{1,0:T(8,128)S(1)}, f32[72,128]{1,0:T(8,128)S(1)}, u32[]{:S(2)}, u32[]{:S(2)}) collective-permute-start(f32[72,128]{1,0:T(8,128)S(1)} %get-tuple-element.120.refs_0_), channel_id=1, source_target_pairs={{0,1},{1,0},{2,3},{3,2},{4,5},{5,4},{6,7},{7,6},{8,9},{9,8},{10,11... | collective-permute-start | bytes 110600 | tf_op jit(solution)/shard_map/ppermute | solution.py:353
  42.1 0.0 copy-done.2
  42.1 2.3 %tile_gradients.3 = (f32[64,128,128]{2,1,0:T(8,128)}, f32[128,128]{1,0:T(8,128)S(1)}, f32[128,256]{1,0:T(8,128)S(1)}) custom-call(f32[128,128]{1,0:T(8,128)S(1)} %bitcast.16, f32[128,64]{1,0:T(8,128)S(1)} %get-tuple-element.110.columns, f32[64,128]{1,0:T(8,128)S(1)} %get-tuple-element.117.survival, f32[64,128,128]{2,1,0:T(8,128)S(1)} %get-tuple-element.101.held, ...), custom_call_target="tpu_custom_call" | custom-call | tf_op jit(solution)/shard_map/tile_gradients/pallas_call | solution.py:339
  44.4 0.0 collective-permute-done.10.refs_2_
  44.4 0.2 collective-permute-done.11.refs_3_
  44.6 0.0 collective-permute-done.9.refs_1_
  44.6 0.8 %last_update.3 = (f32[128,128]{1,0:T(8,128)}, f32[128,128]{1,0:T(8,128)}, s32[1]{0:T(128)S(4)}) custom-call(f32[128,128]{1,0:T(8,128)S(1)} %get-tuple-element.118.current, f32[128,256]{1,0:T(8,128)S(1)} %get-tuple-element.119.hits, f32[72,128]{1,0:T(8,128)S(1)} %get-tuple-element.120.refs_0_, f32[72,128]{1,0:T(8,128)S(1)} %collective-permute-done.9.refs_1_, ...), custom_call_target="tpu_custom_call" | custom-call | tf_op jit(solution)/shard_map/last_update/pallas_call | solution.py:339
  (2 shorter events, 0.0 us)
Async XLA Ops:
  22.9 3.7 %collective-permute-start.6 = (f32[72,128]{1,0:T(8,128)S(1)}, f32[72,128]{1,0:T(8,128)S(1)}, u32[]{:S(2)}, u32[]{:S(2)}) collective-permute-start(f32[72,128]{1,0:T(8,128)S(1)} %gradient.3.after.refs_3_.refs_0_), channel_id=1, source_target_pairs={{0,3},{1,2},{2,1},{3,0},{4,7},{5,6},{6,5},{7,4},{8,11},{9,10},{10,... | collective-permute-start | bytes 110600 | tf_op jit(solution)/shard_map/ppermute | solution.py:353
  22.9 4.2 %collective-permute-start.7 = (f32[72,128]{1,0:T(8,128)S(1)}, f32[72,128]{1,0:T(8,128)S(1)}, u32[]{:S(2)}, u32[]{:S(2)}) collective-permute-start(f32[72,128]{1,0:T(8,128)S(1)} %gradient.3.after.refs_3_.refs_0_), channel_id=1, source_target_pairs={{0,2},{1,3},{2,0},{3,1},{4,6},{5,7},{6,4},{7,5},{8,10},{9,11},{10,... | collective-permute-start | bytes 110600 | tf_op jit(solution)/shard_map/ppermute | solution.py:353
  24.5 2.6 %collective-permute-start.8 = (f32[72,128]{1,0:T(8,128)S(1)}, f32[72,128]{1,0:T(8,128)S(1)}, u32[]{:S(2)}, u32[]{:S(2)}) collective-permute-start(f32[72,128]{1,0:T(8,128)S(1)} %gradient.3.after.refs_3_.refs_0_), channel_id=1, source_target_pairs={{0,1},{1,0},{2,3},{3,2},{4,5},{5,4},{6,7},{7,6},{8,9},{9,8},{10,11... | collective-permute-start | bytes 110600 | tf_op jit(solution)/shard_map/ppermute | solution.py:353
  27.1 15.0 %copy-start.2 = (f32[16384]{0:T(1024)S(1)}, f32[16384]{0:T(1024)}, u32[]{:S(2)}) copy-start(f32[16384]{0:T(1024)} %param.8) | copy-start | bytes 196612
  40.1 4.2 %collective-permute-start.10 = (f32[72,128]{1,0:T(8,128)S(1)}, f32[72,128]{1,0:T(8,128)S(1)}, u32[]{:S(2)}, u32[]{:S(2)}) collective-permute-start(f32[72,128]{1,0:T(8,128)S(1)} %get-tuple-element.120.refs_0_), channel_id=1, source_target_pairs={{0,3},{1,2},{2,1},{3,0},{4,7},{5,6},{6,5},{7,4},{8,11},{9,10},{10,... | collective-permute-start | bytes 110600 | tf_op jit(solution)/shard_map/ppermute | solution.py:353
  40.2 4.4 %collective-permute-start.11 = (f32[72,128]{1,0:T(8,128)S(1)}, f32[72,128]{1,0:T(8,128)S(1)}, u32[]{:S(2)}, u32[]{:S(2)}) collective-permute-start(f32[72,128]{1,0:T(8,128)S(1)} %get-tuple-element.120.refs_0_), channel_id=1, source_target_pairs={{0,2},{1,3},{2,0},{3,1},{4,6},{5,7},{6,4},{7,5},{8,10},{9,11},{10,... | collective-permute-start | bytes 110600 | tf_op jit(solution)/shard_map/ppermute | solution.py:353
  41.1 3.4 %collective-permute-start.9 = (f32[72,128]{1,0:T(8,128)S(1)}, f32[72,128]{1,0:T(8,128)S(1)}, u32[]{:S(2)}, u32[]{:S(2)}) collective-permute-start(f32[72,128]{1,0:T(8,128)S(1)} %get-tuple-element.120.refs_0_), channel_id=1, source_target_pairs={{0,1},{1,0},{2,3},{3,2},{4,5},{5,4},{6,7},{7,6},{8,9},{9,8},{10,11... | collective-permute-start | bytes 110600 | tf_op jit(solution)/shard_map/ppermute | solution.py:353

commit v6 on v5

--- a/solution.py
+++ b/solution.py
@@ -12,7 +12,7 @@
 CHUNK = 8
 FEW = 16
 HALVES = 2
-SHARED = 3
+SHARED = 2
 F32 = jnp.float32
 BF16 = jnp.bfloat16
 
@@ -215,7 +215,7 @@
     total = jnp.zeros((width, width), F32)
     for s in range(slots):
         terms = ratios[s] * survival[s : s + 1, :]
-        if s % 3 == 2:
+        if s % 2 == 1:
             high = terms.astype(BF16)
             low = (terms - high.astype(F32)).astype(BF16)
             sums = jnp.dot(high, ones, preferred_element_type=F32) + jnp.dot(low, ones, preferred_element_type=F32)

time: 45.6 us -> 45.4 us (level)
  transfers between devices with their start and end apart: 6 -> 6, of which waited for: 3 -> 3; matrix products, arithmetic and copies ran while one was open for 0% -> 0% of each run, Pallas kernels for 6% -> 7%
where the time goes in v6:
time: 45.4 us; the launch traced here: 45.1 us
  blocking collectives  27.8 us (61%)
  Pallas kernels  10.3 us (23%)
  starting transfers between devices  3.82 us (8%)
  waiting for transfers between devices  1.87 us (4%)
  between operations  1.35 us (3%)
    all_to_all x1, blocking collectives, over_tests(): lax.all_to_all(jnp.broadcast_to(x[None], (tests,) + x.shape), 'tests', 0, 0)  17.4 us
    all_to_all x1, blocking collectives, sweep(): received = lax.all_to_all(rows, 'tests', 0, 0)  10.4 us
    pallas_call x8, Pallas kernels, call(): pl.pallas_call(kernel, out_shape=outs, in_specs=more.pop('in_specs', [VME...  10.3 us
    ppermute x6, starting transfers between devices, over_branches(): lax.ppermute(x, 'branches', [(b, b ^ k) for b in range(branches)])  3.82 us
    ppermute x6, waiting for transfers between devices, over_branches(): lax.ppermute(x, 'branches', [(b, b ^ k) for b in range(branches)])  1.87 us
  transfers between devices with their start and end apart: 6, of which 3 were waited for; matrix products, arithmetic and copies ran while one was open for 0% of the time, Pallas kernels for 7%

profile of v6, /device:TPU:0, one launch (start us, length us, event | category | flops | bytes accessed | tf_op | source)
XLA Modules:
  0.0 45.1 jit_solution(11620120632270859602)
XLA Ops:
  1.3 3.0 %first_logs.3 = (f32[72,128]{1,0:T(8,128)S(1)}, f32[64,128,128]{2,1,0:T(8,128)S(1)}, f32[64,128,128]{2,1,0:T(8,128)S(1)}, f32[64,128]{1,0:T(8,128)S(1)}, f32[8,1...) custom-call(s32[1]{0:T(128)S(6)} %copy.22.limit, s32[1,64]{1,0:T(1,128)} %bitcast.19, ...), custom_call_target="tpu_custom_call" | custom-call | tf_op jit(solution)/shard_map/first_logs/pallas_call | solution.py:339
  4.3 17.4 %all_to_all.20.gathered.others = f32[8,72,128]{2,1,0:T(8,128)S(1)} all-to-all(f32[8,72,128]{2,1,0:T(8,128)S(1)} %broadcast_in_dim.6), channel_id=1, replica_groups=mesh['tests'=8,'branches'=4] {'tests'}, dimensions={0} | all-to-all | bytes 589824 | tf_op jit(solution)/shard_map/all_to_all | solution.py:350
  21.7 1.0 %gradient.3.after.refs_3_.refs_0_ = f32[72,128]{1,0:T(8,128)S(1)} custom-call(f32[8,72,128]{2,1,0:T(8,128)S(1)} %all_to_all.20.gathered.others, f32[64,128]{1,0:T(8,128)S(1)} %get-tuple-element.105.mine, f32[64,128]{1,0:T(8,128)S(1)} %get-tuple-element.106.slot_weights, f32[64,128,128]{2,1,0:T(8,128)S(1)} %get-tuple-element.107.ratios, ...), custom_call_target="tpu_custom_call" | custom-call | tf_op jit(solution)/shard_map/gradient/pallas_call | solution.py:339
  22.7 0.1 collective-permute-start.6
  22.8 1.6 %collective-permute-start.7 = (f32[72,128]{1,0:T(8,128)S(1)}, f32[72,128]{1,0:T(8,128)S(1)}, u32[]{:S(2)}, u32[]{:S(2)}) collective-permute-start(f32[72,128]{1,0:T(8,128)S(1)} %gradient.3.after.refs_3_.refs_0_), channel_id=1, source_target_pairs={{0,2},{1,3},{2,0},{3,1},{4,6},{5,7},{6,4},{7,5},{8,10},{9,11},{10,... | collective-permute-start | bytes 110600 | tf_op jit(solution)/shard_map/ppermute | solution.py:353
  24.4 0.3 collective-permute-start.8
  24.6 0.7 %plan.1 = (f32[8,128]{1,0:T(8,128)S(1)}, f32[128,64]{1,0:T(8,128)S(1)}, f32[64,128]{1,0:T(8,128)S(1)}, f32[64,64]{1,0:T(8,128)S(1)}) custom-call(f32[8,72,128]{2,1,0:T(8,128)S(1)} %all_to_all.20.gathered.others, f32[64,128]{1,0:T(8,128)S(1)} %get-tuple-element.105.mine, f32[72,128]{1,0:T(8,128)S(1)} %get-tuple-element.104.payload, ...), custom_call_target="tpu_custom_call" | custom-call | tf_op jit(solution)/shard_map/plan/pallas_call | solution.py:339
  25.3 1.2 %collective-permute-done.6.refs_0_.refs_3_ = f32[72,128]{1,0:T(8,128)S(1)} collective-permute-done((f32[72,128]{1,0:T(8,128)S(1)}, f32[72,128]{1,0:T(8,128)S(1)}, u32[]{:S(2)}, u32[]{:S(2)}) %collective-permute-start.6) | collective-permute-done | bytes 36896 | tf_op jit(solution)/shard_map/ppermute | solution.py:353
  26.5 0.5 %collective-permute-done.7.refs_1_.refs_2_ = f32[72,128]{1,0:T(8,128)S(1)} collective-permute-done((f32[72,128]{1,0:T(8,128)S(1)}, f32[72,128]{1,0:T(8,128)S(1)}, u32[]{:S(2)}, u32[]{:S(2)}) %collective-permute-start.7) | collective-permute-done | bytes 36896 | tf_op jit(solution)/shard_map/ppermute | solution.py:353
  26.9 0.0 collective-permute-done.8.refs_2_.refs_1_
  26.9 0.0 copy-start.2
  26.9 1.5 %next_logs.3 = (f32[128,64]{1,0:T(8,128)S(1)}, f32[64,128]{1,0:T(8,128)S(1)}, f32[64,128,128]{2,1,0:T(8,128)S(1)}, f32[8,16,128]{2,1,0:T(8,128)S(1)}) custom-call(f32[64,128,128]{2,1,0:T(8,128)S(1)} %get-tuple-element.101.held, f32[64,128]{1,0:T(8,128)S(1)} %get-tuple-element.102.down, f32[64,128]{1,0:T(8,128)S(1)} %get-tuple-element.103.picked, ...), custom_call_target="tpu_custom_call" | custom-call | tf_op jit(solution)/shard_map/next_logs/pallas_call | solution.py:339
  28.4 10.4 %all_to_all.21.received = f32[8,16,128]{2,1,0:T(8,128)S(1)} all-to-all(f32[8,16,128]{2,1,0:T(8,128)S(1)} %get-tuple-element.111), channel_id=1, replica_groups=mesh['tests'=8,'branches'=4] {'tests'}, dimensions={0} | all-to-all | bytes 131072 | tf_op jit(solution)/shard_map/all_to_all | solution.py:395
  38.8 0.2 few_rows.1.total
  39.0 0.8 %last_gradient.3 = (f32[72,128]{1,0:T(8,128)S(1)}, f32[64,128]{1,0:T(8,128)S(1)}) custom-call(f32[64,128]{1,0:T(8,128)S(1)} %few_rows.1.total, f32[64,128]{1,0:T(8,128)S(1)} %get-tuple-element.106.slot_weights, f32[64,128,128]{2,1,0:T(8,128)S(1)} %get-tuple-element.115.ratios, f32[8,128]{1,0:T(8,128)S(1)} %get-tuple-element.116.few), custom_call_target="tpu_custom_call" | custom-call | tf_op jit(solution)/shard_map/last_gradient/pallas_call | solution.py:339
  39.9 0.1 collective-permute-start.10
  39.9 0.9 %collective-permute-start.11 = (f32[72,128]{1,0:T(8,128)S(1)}, f32[72,128]{1,0:T(8,128)S(1)}, u32[]{:S(2)}, u32[]{:S(2)}) collective-permute-start(f32[72,128]{1,0:T(8,128)S(1)} %get-tuple-element.120.refs_0_), channel_id=1, source_target_pairs={{0,2},{1,3},{2,0},{3,1},{4,6},{5,7},{6,4},{7,5},{8,10},{9,11},{10,... | collective-permute-start | bytes 110600 | tf_op jit(solution)/shard_map/ppermute | solution.py:353
  40.9 0.9 %collective-permute-start.9 = (f32[72,128]{1,0:T(8,128)S(1)}, f32[72,128]{1,0:T(8,128)S(1)}, u32[]{:S(2)}, u32[]{:S(2)}) collective-permute-start(f32[72,128]{1,0:T(8,128)S(1)} %get-tuple-element.120.refs_0_), channel_id=1, source_target_pairs={{0,1},{1,0},{2,3},{3,2},{4,5},{5,4},{6,7},{7,6},{8,9},{9,8},{10,11... | collective-permute-start | bytes 110600 | tf_op jit(solution)/shard_map/ppermute | solution.py:353
  41.8 0.0 copy-done.2
  41.8 2.3 %tile_gradients.3 = (f32[64,128,128]{2,1,0:T(8,128)}, f32[128,128]{1,0:T(8,128)S(1)}, f32[128,256]{1,0:T(8,128)S(1)}) custom-call(f32[128,128]{1,0:T(8,128)S(1)} %bitcast.16, f32[128,64]{1,0:T(8,128)S(1)} %get-tuple-element.110.columns, f32[64,128]{1,0:T(8,128)S(1)} %get-tuple-element.117.survival, f32[64,128,128]{2,1,0:T(8,128)S(1)} %get-tuple-element.101.held, ...), custom_call_target="tpu_custom_call" | custom-call | tf_op jit(solution)/shard_map/tile_gradients/pallas_call | solution.py:339
  44.1 0.0 collective-permute-done.10.refs_2_
  44.1 0.2 collective-permute-done.11.refs_3_
  44.3 0.0 collective-permute-done.9.refs_1_
  44.3 0.8 %last_update.3 = (f32[128,128]{1,0:T(8,128)}, f32[128,128]{1,0:T(8,128)}, s32[1]{0:T(128)S(4)}) custom-call(f32[128,128]{1,0:T(8,128)S(1)} %get-tuple-element.118.current, f32[128,256]{1,0:T(8,128)S(1)} %get-tuple-element.119.hits, f32[72,128]{1,0:T(8,128)S(1)} %get-tuple-element.120.refs_0_, f32[72,128]{1,0:T(8,128)S(1)} %collective-permute-done.9.refs_1_, ...), custom_call_target="tpu_custom_call" | custom-call | tf_op jit(solution)/shard_map/last_update/pallas_call | solution.py:339
  (2 shorter events, 0.0 us)
Async XLA Ops:
  22.7 3.8 %collective-permute-start.6 = (f32[72,128]{1,0:T(8,128)S(1)}, f32[72,128]{1,0:T(8,128)S(1)}, u32[]{:S(2)}, u32[]{:S(2)}) collective-permute-start(f32[72,128]{1,0:T(8,128)S(1)} %gradient.3.after.refs_3_.refs_0_), channel_id=1, source_target_pairs={{0,3},{1,2},{2,1},{3,0},{4,7},{5,6},{6,5},{7,4},{8,11},{9,10},{10,... | collective-permute-start | bytes 110600 | tf_op jit(solution)/shard_map/ppermute | solution.py:353
  22.8 4.2 %collective-permute-start.7 = (f32[72,128]{1,0:T(8,128)S(1)}, f32[72,128]{1,0:T(8,128)S(1)}, u32[]{:S(2)}, u32[]{:S(2)}) collective-permute-start(f32[72,128]{1,0:T(8,128)S(1)} %gradient.3.after.refs_3_.refs_0_), channel_id=1, source_target_pairs={{0,2},{1,3},{2,0},{3,1},{4,6},{5,7},{6,4},{7,5},{8,10},{9,11},{10,... | collective-permute-start | bytes 110600 | tf_op jit(solution)/shard_map/ppermute | solution.py:353
  24.4 2.6 %collective-permute-start.8 = (f32[72,128]{1,0:T(8,128)S(1)}, f32[72,128]{1,0:T(8,128)S(1)}, u32[]{:S(2)}, u32[]{:S(2)}) collective-permute-start(f32[72,128]{1,0:T(8,128)S(1)} %gradient.3.after.refs_3_.refs_0_), channel_id=1, source_target_pairs={{0,1},{1,0},{2,3},{3,2},{4,5},{5,4},{6,7},{7,6},{8,9},{9,8},{10,11... | collective-permute-start | bytes 110600 | tf_op jit(solution)/shard_map/ppermute | solution.py:353
  26.9 14.8 %copy-start.2 = (f32[16384]{0:T(1024)S(1)}, f32[16384]{0:T(1024)}, u32[]{:S(2)}) copy-start(f32[16384]{0:T(1024)} %param.8) | copy-start | bytes 196612
  39.9 4.2 %collective-permute-start.10 = (f32[72,128]{1,0:T(8,128)S(1)}, f32[72,128]{1,0:T(8,128)S(1)}, u32[]{:S(2)}, u32[]{:S(2)}) collective-permute-start(f32[72,128]{1,0:T(8,128)S(1)} %get-tuple-element.120.refs_0_), channel_id=1, source_target_pairs={{0,3},{1,2},{2,1},{3,0},{4,7},{5,6},{6,5},{7,4},{8,11},{9,10},{10,... | collective-permute-start | bytes 110600 | tf_op jit(solution)/shard_map/ppermute | solution.py:353
  39.9 4.4 %collective-permute-start.11 = (f32[72,128]{1,0:T(8,128)S(1)}, f32[72,128]{1,0:T(8,128)S(1)}, u32[]{:S(2)}, u32[]{:S(2)}) collective-permute-start(f32[72,128]{1,0:T(8,128)S(1)} %get-tuple-element.120.refs_0_), channel_id=1, source_target_pairs={{0,2},{1,3},{2,0},{3,1},{4,6},{5,7},{6,4},{7,5},{8,10},{9,11},{10,... | collective-permute-start | bytes 110600 | tf_op jit(solution)/shard_map/ppermute | solution.py:353
  40.9 3.4 %collective-permute-start.9 = (f32[72,128]{1,0:T(8,128)S(1)}, f32[72,128]{1,0:T(8,128)S(1)}, u32[]{:S(2)}, u32[]{:S(2)}) collective-permute-start(f32[72,128]{1,0:T(8,128)S(1)} %get-tuple-element.120.refs_0_), channel_id=1, source_target_pairs={{0,1},{1,0},{2,3},{3,2},{4,5},{5,4},{6,7},{7,6},{8,9},{9,8},{10,11... | collective-permute-start | bytes 110600 | tf_op jit(solution)/shard_map/ppermute | solution.py:353

commit v7 on v6

--- a/solution.py
+++ b/solution.py
@@ -152,9 +152,12 @@
     out[...] = log_survival(gathered, others, mine)
 
 
-def few_rows_kernel(received, places, own, logs, out):
-    others = pick(places[...].astype(BF16), received[...].reshape(-1, received.shape[-1]))
-    out[...] = others + pick(own[...].astype(BF16), logs[...])
+def few_rows_kernel(received, places, own, logs, slot_weights, ratios, few, out, survival):
+    rows = jnp.concatenate([received[...].reshape(-1, received.shape[-1]), logs[...]], axis=0)
+    total = pick(jnp.concatenate([places[...], own[...]], axis=1).astype(BF16), rows)
+    survival[...] = slot_weights[...] * jnp.exp(total)
+    slot_sums(survival[...], ratios, out)
+    out[slot_weights.shape[0] :, :] = few[...]
 
 
 def before_in(shape, slots):
@@ -393,7 +396,9 @@
             scratch_shapes=[products],
         )
         received = lax.all_to_all(rows, "tests", 0, 0)
-        total = call(few_rows_kernel, per_slot, (received, places, own, logs), "few_rows")
+        sums, survival = call(
+            few_rows_kernel, (labelled, per_slot), (received, places, own, logs, slot_weights, ratios, few), "last_gradient"
+        )
     else:
         few = jnp.ones(label.shape, F32)
         columns, logs, ratios = call(
@@ -404,9 +409,9 @@
             scratch_shapes=[products],
         )
         total = call(all_rows_kernel, per_slot, (over_tests(logs), others, mine), "all_rows")
-    sums, survival = call(
-        last_gradient_kernel, (labelled, per_slot), (total, slot_weights, ratios, few), "last_gradient"
-    )
+        sums, survival = call(
+            last_gradient_kernel, (labelled, per_slot), (total, slot_weights, ratios, few), "last_gradient"
+        )
     last_parts = over_branches(sums)
     part_rows = pltpu.VMEM((branches, slots, width), F32)
     tile_grads, current, hits = call(

time: 45.4 us -> 45.3 us (level)
    pallas_call x8 -> x7, Pallas kernels: 10.3 us -> 10.2 us  [call(): pl.pallas_call(kernel, out_shape=outs, in_specs=more.pop('in_specs', [VME...]
where the time goes in v7:
time: 45.3 us; the launch traced here: 45.1 us
  blocking collectives  27.8 us (61%)
  Pallas kernels  10.2 us (23%)
  starting transfers between devices  3.82 us (8%)
  waiting for transfers between devices  1.87 us (4%)
  between operations  1.34 us (3%)
    all_to_all x1, blocking collectives, over_tests(): lax.all_to_all(jnp.broadcast_to(x[None], (tests,) + x.shape), 'tests', 0, 0)  17.4 us
    all_to_all x1, blocking collectives, sweep(): received = lax.all_to_all(rows, 'tests', 0, 0)  10.4 us
    pallas_call x7, Pallas kernels, call(): pl.pallas_call(kernel, out_shape=outs, in_specs=more.pop('in_specs', [VME...  10.2 us
    ppermute x6, starting transfers between devices, over_branches(): lax.ppermute(x, 'branches', [(b, b ^ k) for b in range(branches)])  3.82 us
    ppermute x6, waiting for transfers between devices, over_branches(): lax.ppermute(x, 'branches', [(b, b ^ k) for b in range(branches)])  1.87 us
  transfers between devices with their start and end apart: 6, of which 3 were waited for; matrix products, arithmetic and copies ran while one was open for 0% of the time, Pallas kernels for 7%

profile of v7, /device:TPU:0, one launch (start us, length us, event | category | flops | bytes accessed | tf_op | source)
XLA Modules:
  0.0 45.1 jit_solution(9114535368235367452)
XLA Ops:
  1.3 3.0 %first_logs.3 = (f32[72,128]{1,0:T(8,128)S(1)}, f32[64,128,128]{2,1,0:T(8,128)S(1)}, f32[64,128,128]{2,1,0:T(8,128)S(1)}, f32[64,128]{1,0:T(8,128)S(1)}, f32[8,1...) custom-call(s32[1]{0:T(128)S(6)} %copy.22.limit, s32[1,64]{1,0:T(1,128)} %bitcast.19, ...), custom_call_target="tpu_custom_call" | custom-call | tf_op jit(solution)/shard_map/first_logs/pallas_call | solution.py:342
  4.3 17.4 %all_to_all.20.gathered.others = f32[8,72,128]{2,1,0:T(8,128)S(1)} all-to-all(f32[8,72,128]{2,1,0:T(8,128)S(1)} %broadcast_in_dim.6), channel_id=1, replica_groups=mesh['tests'=8,'branches'=4] {'tests'}, dimensions={0} | all-to-all | bytes 589824 | tf_op jit(solution)/shard_map/all_to_all | solution.py:353
  21.7 1.0 %gradient.3.after.refs_3_.refs_0_ = f32[72,128]{1,0:T(8,128)S(1)} custom-call(f32[8,72,128]{2,1,0:T(8,128)S(1)} %all_to_all.20.gathered.others, f32[64,128]{1,0:T(8,128)S(1)} %get-tuple-element.105.mine, f32[64,128]{1,0:T(8,128)S(1)} %get-tuple-element.106.slot_weights, f32[64,128,128]{2,1,0:T(8,128)S(1)} %get-tuple-element.107.ratios, ...), custom_call_target="tpu_custom_call" | custom-call | tf_op jit(solution)/shard_map/gradient/pallas_call | solution.py:342
  22.7 0.1 collective-permute-start.6
  22.8 1.6 %collective-permute-start.7 = (f32[72,128]{1,0:T(8,128)S(1)}, f32[72,128]{1,0:T(8,128)S(1)}, u32[]{:S(2)}, u32[]{:S(2)}) collective-permute-start(f32[72,128]{1,0:T(8,128)S(1)} %gradient.3.after.refs_3_.refs_0_), channel_id=1, source_target_pairs={{0,2},{1,3},{2,0},{3,1},{4,6},{5,7},{6,4},{7,5},{8,10},{9,11},{10,... | collective-permute-start | bytes 110600 | tf_op jit(solution)/shard_map/ppermute | solution.py:356
  24.4 0.3 collective-permute-start.8
  24.6 0.7 %plan.1 = (f32[8,128]{1,0:T(8,128)S(1)}, f32[128,64]{1,0:T(8,128)S(1)}, f32[64,128]{1,0:T(8,128)S(1)}, f32[64,64]{1,0:T(8,128)S(1)}) custom-call(f32[8,72,128]{2,1,0:T(8,128)S(1)} %all_to_all.20.gathered.others, f32[64,128]{1,0:T(8,128)S(1)} %get-tuple-element.105.mine, f32[72,128]{1,0:T(8,128)S(1)} %get-tuple-element.104.payload, ...), custom_call_target="tpu_custom_call" | custom-call | tf_op jit(solution)/shard_map/plan/pallas_call | solution.py:342
  25.3 1.2 %collective-permute-done.6.refs_0_.refs_3_ = f32[72,128]{1,0:T(8,128)S(1)} collective-permute-done((f32[72,128]{1,0:T(8,128)S(1)}, f32[72,128]{1,0:T(8,128)S(1)}, u32[]{:S(2)}, u32[]{:S(2)}) %collective-permute-start.6) | collective-permute-done | bytes 36896 | tf_op jit(solution)/shard_map/ppermute | solution.py:356
  26.5 0.5 %collective-permute-done.7.refs_1_.refs_2_ = f32[72,128]{1,0:T(8,128)S(1)} collective-permute-done((f32[72,128]{1,0:T(8,128)S(1)}, f32[72,128]{1,0:T(8,128)S(1)}, u32[]{:S(2)}, u32[]{:S(2)}) %collective-permute-start.7) | collective-permute-done | bytes 36896 | tf_op jit(solution)/shard_map/ppermute | solution.py:356
  26.9 0.0 collective-permute-done.8.refs_2_.refs_1_
  26.9 0.0 copy-start.2
  26.9 1.5 %next_logs.3 = (f32[128,64]{1,0:T(8,128)S(1)}, f32[64,128]{1,0:T(8,128)S(1)}, f32[64,128,128]{2,1,0:T(8,128)S(1)}, f32[8,16,128]{2,1,0:T(8,128)S(1)}) custom-call(f32[64,128,128]{2,1,0:T(8,128)S(1)} %get-tuple-element.101.held, f32[64,128]{1,0:T(8,128)S(1)} %get-tuple-element.102.down, f32[64,128]{1,0:T(8,128)S(1)} %get-tuple-element.103.picked, ...), custom_call_target="tpu_custom_call" | custom-call | tf_op jit(solution)/shard_map/next_logs/pallas_call | solution.py:342
  28.4 10.4 %all_to_all.21.received = f32[8,16,128]{2,1,0:T(8,128)S(1)} all-to-all(f32[8,16,128]{2,1,0:T(8,128)S(1)} %get-tuple-element.111), channel_id=1, replica_groups=mesh['tests'=8,'branches'=4] {'tests'}, dimensions={0} | all-to-all | bytes 131072 | tf_op jit(solution)/shard_map/all_to_all | solution.py:398
  38.8 1.0 %last_gradient.3 = (f32[72,128]{1,0:T(8,128)S(1)}, f32[64,128]{1,0:T(8,128)S(1)}) custom-call(f32[8,16,128]{2,1,0:T(8,128)S(1)} %all_to_all.21.received, f32[64,128]{1,0:T(8,128)S(1)} %get-tuple-element.112.places, f32[64,64]{1,0:T(8,128)S(1)} %get-tuple-element.113.own, f32[64,128]{1,0:T(8,128)S(1)} %get-tuple-element.114.logs, ...), custom_call_target="tpu_custom_call" | custom-call | tf_op jit(solution)/shard_map/last_gradient/pallas_call | solution.py:342
  39.8 0.1 collective-permute-start.10
  39.9 0.9 %collective-permute-start.11 = (f32[72,128]{1,0:T(8,128)S(1)}, f32[72,128]{1,0:T(8,128)S(1)}, u32[]{:S(2)}, u32[]{:S(2)}) collective-permute-start(f32[72,128]{1,0:T(8,128)S(1)} %get-tuple-element.120.refs_0_), channel_id=1, source_target_pairs={{0,2},{1,3},{2,0},{3,1},{4,6},{5,7},{6,4},{7,5},{8,10},{9,11},{10,... | collective-permute-start | bytes 110600 | tf_op jit(solution)/shard_map/ppermute | solution.py:356
  40.8 0.9 %collective-permute-start.9 = (f32[72,128]{1,0:T(8,128)S(1)}, f32[72,128]{1,0:T(8,128)S(1)}, u32[]{:S(2)}, u32[]{:S(2)}) collective-permute-start(f32[72,128]{1,0:T(8,128)S(1)} %get-tuple-element.120.refs_0_), channel_id=1, source_target_pairs={{0,1},{1,0},{2,3},{3,2},{4,5},{5,4},{6,7},{7,6},{8,9},{9,8},{10,11... | collective-permute-start | bytes 110600 | tf_op jit(solution)/shard_map/ppermute | solution.py:356
  41.7 0.0 copy-done.2
  41.7 2.3 %tile_gradients.3 = (f32[64,128,128]{2,1,0:T(8,128)}, f32[128,128]{1,0:T(8,128)S(1)}, f32[128,256]{1,0:T(8,128)S(1)}) custom-call(f32[128,128]{1,0:T(8,128)S(1)} %bitcast.16, f32[128,64]{1,0:T(8,128)S(1)} %get-tuple-element.110.columns, f32[64,128]{1,0:T(8,128)S(1)} %get-tuple-element.117.survival, f32[64,128,128]{2,1,0:T(8,128)S(1)} %get-tuple-element.101.held, ...), custom_call_target="tpu_custom_call" | custom-call | tf_op jit(solution)/shard_map/tile_gradients/pallas_call | solution.py:342
  44.0 0.0 collective-permute-done.10.refs_2_
  44.0 0.2 collective-permute-done.11.refs_3_
  44.2 0.0 collective-permute-done.9.refs_1_
  44.2 0.8 %last_update.3 = (f32[128,128]{1,0:T(8,128)}, f32[128,128]{1,0:T(8,128)}, s32[1]{0:T(128)S(4)}) custom-call(f32[128,128]{1,0:T(8,128)S(1)} %get-tuple-element.118.current, f32[128,256]{1,0:T(8,128)S(1)} %get-tuple-element.119.hits, f32[72,128]{1,0:T(8,128)S(1)} %get-tuple-element.120.refs_0_, f32[72,128]{1,0:T(8,128)S(1)} %collective-permute-done.9.refs_1_, ...), custom_call_target="tpu_custom_call" | custom-call | tf_op jit(solution)/shard_map/last_update/pallas_call | solution.py:342
  (2 shorter events, 0.0 us)
Async XLA Ops:
  22.7 3.8 %collective-permute-start.6 = (f32[72,128]{1,0:T(8,128)S(1)}, f32[72,128]{1,0:T(8,128)S(1)}, u32[]{:S(2)}, u32[]{:S(2)}) collective-permute-start(f32[72,128]{1,0:T(8,128)S(1)} %gradient.3.after.refs_3_.refs_0_), channel_id=1, source_target_pairs={{0,3},{1,2},{2,1},{3,0},{4,7},{5,6},{6,5},{7,4},{8,11},{9,10},{10,... | collective-permute-start | bytes 110600 | tf_op jit(solution)/shard_map/ppermute | solution.py:356
  22.8 4.2 %collective-permute-start.7 = (f32[72,128]{1,0:T(8,128)S(1)}, f32[72,128]{1,0:T(8,128)S(1)}, u32[]{:S(2)}, u32[]{:S(2)}) collective-permute-start(f32[72,128]{1,0:T(8,128)S(1)} %gradient.3.after.refs_3_.refs_0_), channel_id=1, source_target_pairs={{0,2},{1,3},{2,0},{3,1},{4,6},{5,7},{6,4},{7,5},{8,10},{9,11},{10,... | collective-permute-start | bytes 110600 | tf_op jit(solution)/shard_map/ppermute | solution.py:356
  24.4 2.6 %collective-permute-start.8 = (f32[72,128]{1,0:T(8,128)S(1)}, f32[72,128]{1,0:T(8,128)S(1)}, u32[]{:S(2)}, u32[]{:S(2)}) collective-permute-start(f32[72,128]{1,0:T(8,128)S(1)} %gradient.3.after.refs_3_.refs_0_), channel_id=1, source_target_pairs={{0,1},{1,0},{2,3},{3,2},{4,5},{5,4},{6,7},{7,6},{8,9},{9,8},{10,11... | collective-permute-start | bytes 110600 | tf_op jit(solution)/shard_map/ppermute | solution.py:356
  26.9 14.8 %copy-start.2 = (f32[16384]{0:T(1024)S(1)}, f32[16384]{0:T(1024)}, u32[]{:S(2)}) copy-start(f32[16384]{0:T(1024)} %param.8) | copy-start | bytes 196612
  39.8 4.2 %collective-permute-start.10 = (f32[72,128]{1,0:T(8,128)S(1)}, f32[72,128]{1,0:T(8,128)S(1)}, u32[]{:S(2)}, u32[]{:S(2)}) collective-permute-start(f32[72,128]{1,0:T(8,128)S(1)} %get-tuple-element.120.refs_0_), channel_id=1, source_target_pairs={{0,3},{1,2},{2,1},{3,0},{4,7},{5,6},{6,5},{7,4},{8,11},{9,10},{10,... | collective-permute-start | bytes 110600 | tf_op jit(solution)/shard_map/ppermute | solution.py:356
  39.9 4.4 %collective-permute-start.11 = (f32[72,128]{1,0:T(8,128)S(1)}, f32[72,128]{1,0:T(8,128)S(1)}, u32[]{:S(2)}, u32[]{:S(2)}) collective-permute-start(f32[72,128]{1,0:T(8,128)S(1)} %get-tuple-element.120.refs_0_), channel_id=1, source_target_pairs={{0,2},{1,3},{2,0},{3,1},{4,6},{5,7},{6,4},{7,5},{8,10},{9,11},{10,... | collective-permute-start | bytes 110600 | tf_op jit(solution)/shard_map/ppermute | solution.py:356
  40.8 3.4 %collective-permute-start.9 = (f32[72,128]{1,0:T(8,128)S(1)}, f32[72,128]{1,0:T(8,128)S(1)}, u32[]{:S(2)}, u32[]{:S(2)}) collective-permute-start(f32[72,128]{1,0:T(8,128)S(1)} %get-tuple-element.120.refs_0_), channel_id=1, source_target_pairs={{0,1},{1,0},{2,3},{3,2},{4,5},{5,4},{6,7},{7,6},{8,9},{9,8},{10,11... | collective-permute-start | bytes 110600 | tf_op jit(solution)/shard_map/ppermute | solution.py:356
